TPU v7x, 512 devices: a whole 4x8x8 slice. The times are simulated.
512 devices in a mesh: page: 64 (over x, z, core), tensor: 8 (over y).
Axes of the slice: x: 4, y: 8, z: 8, core: 2. Of those that a mesh axis runs over, the one named last changes fastest.
Arguments:
- queries: bfloat16 [128, 4, 8192], P('page', None, 'tensor'), may hold values from -8 to 8
- prompt_keys: bfloat16 [65536, 1024], P('page', 'tensor'), may hold values from -8 to 8
- prompt_values: bfloat16 [65536, 1024], P('page', 'tensor'), may hold values from -6 to 6
- pool_keys: bfloat16 [65536, 1024], P('page', 'tensor'), may hold values from -6 to 6
- pool_values: bfloat16 [65536, 1024], P('page', 'tensor'), may hold values from -6 to 6
- suffix_keys: bfloat16 [128, 512, 1024], P('page', None, 'tensor'), may hold values from -10 to 10
- suffix_values: bfloat16 [128, 512, 1024], P('page', None, 'tensor'), may hold values from -6 to 6
- new_keys: bfloat16 [128, 4, 1024], P('page', None, 'tensor'), may hold values from -14 to 14
- new_values: bfloat16 [128, 4, 1024], P('page', None, 'tensor'), may hold values from -6 to 6
- suffix_lengths: int32 [128], P('page'), may hold values from 1 to 512, as said below
- branch_group: int32 [128], replicated, may hold values from 0 to 15
- page_list: int32 [16, 16], replicated, may hold values from 0 to 255, as said below
- out_weight: bfloat16 [8192, 5120], P('tensor', 'page'), may hold values from -0.0625 to 0.0625
Outputs:
- projected: bfloat16 [512, 5120], P('tensor', 'page')
Inputs may be any that keep to these rules, and one draw needn't show every extreme that they name: `suffix_lengths`: some branch has 512 live suffix tokens and some branch has one. `page_list`: every pool page is listed exactly once over all groups.
All inputs are finite; a program needn't handle non-finite values.
Results may differ from a plain program's by a relative error of at most 0.0058.
Values may be sent and summed in bfloat16 or wider, within the bound.
No kernel may reach another device: no remote copies, remote signals or barrier semaphores. Data moves between devices by JAX's collectives and lax.ppermute only.
A program may use at most 64 MiB of HBM per device.

v0:
```python
import math

import jax
import jax.numpy as jnp
from jax import lax
from jax.sharding import PartitionSpec as P

HD = 128
PAGE = 256


def partial_block(query_rows, key_rows, value_rows, allowed, factor):
    scores = (
        jnp.einsum("bskgd,bnkd->bskgn", query_rows, key_rows, preferred_element_type=jnp.float32)
        * factor
    )
    scores = jnp.where(allowed[:, :, None, None, :], scores, -jnp.inf)
    maxima = jnp.max(scores, axis=-1)
    powers = jnp.exp(scores - maxima[..., None])
    totals = jnp.sum(powers, axis=-1)
    outputs = jnp.einsum(
        "bskgn,bnkd->bskgd",
        powers.astype(jnp.bfloat16),
        value_rows,
        preferred_element_type=jnp.float32,
    )
    normed = (outputs / totals[..., None]).astype(jnp.bfloat16)
    return (normed, maxima + jnp.log(totals))


def local(
    queries,
    prompt_keys,
    prompt_values,
    pool_keys,
    pool_values,
    suffix_keys,
    suffix_values,
    new_keys,
    new_values,
    suffix_lengths,
    branch_group,
    page_list,
    out_weight,
):
    owned, steps, width = queries.shape
    kv_local = prompt_keys.shape[1] // HD
    heads_local = width // HD
    group_size = heads_local // kv_local
    factor = 1.0 / math.sqrt(HD)
    pages = lax.axis_size("page")
    rows_local = owned * steps
    rows_all = rows_local * pages
    gathered = lax.all_gather(queries, "page", axis=0, tiled=True)
    query_all = gathered.reshape(1, rows_all, kv_local, group_size, HD)
    row_group = jnp.repeat(branch_group, steps)
    pages_here = pool_keys.shape[0] // PAGE
    device_index = lax.axis_index("page")
    page_ids = device_index * pages_here + jnp.arange(pages_here)
    matched = page_list[:, :, None] == page_ids[None, None, :]
    owner_group = jnp.sum(
        jnp.where(matched, jnp.arange(page_list.shape[0])[:, None, None], 0), axis=(0, 1)
    )
    token_group = jnp.repeat(owner_group, PAGE)
    prompt_len = prompt_keys.shape[0]
    key_rows = jnp.concatenate([prompt_keys, pool_keys], axis=0).reshape(1, -1, kv_local, HD)
    value_rows = jnp.concatenate([prompt_values, pool_values], axis=0).reshape(1, -1, kv_local, HD)
    block_rows = 64

    def one_block(offset):
        query_block = lax.dynamic_slice_in_dim(query_all, offset, block_rows, 1)
        group_block = lax.dynamic_slice_in_dim(row_group, offset, block_rows, 0)
        visible = jnp.concatenate(
            [
                jnp.ones((block_rows, prompt_len), dtype=bool),
                group_block[:, None] == token_group[None, :],
            ],
            axis=1,
        )[None]
        return partial_block(query_block, key_rows, value_rows, visible, factor)

    normed, lse = lax.map(one_block, jnp.arange(rows_all // block_rows) * block_rows)
    normed = normed.reshape(pages, rows_local, heads_local, HD)
    lse = lse.reshape(pages, rows_local, heads_local)
    suffix_len = suffix_keys.shape[1]
    own_query = queries.reshape(owned, steps, kv_local, group_size, HD)
    own_keys = jnp.concatenate([suffix_keys, new_keys], axis=1).reshape(
        owned, suffix_len + steps, kv_local, HD
    )
    own_values = jnp.concatenate([suffix_values, new_values], axis=1).reshape(
        owned, suffix_len + steps, kv_local, HD
    )
    old_allowed = jnp.arange(suffix_len)[None, None, :] < suffix_lengths[:, None, None]
    new_allowed = jnp.arange(steps)[None, :, None] >= jnp.arange(steps)[None, None, :]
    allowed = jnp.concatenate(
        [
            jnp.broadcast_to(old_allowed, (owned, steps, suffix_len)),
            jnp.broadcast_to(new_allowed, (owned, steps, steps)),
        ],
        axis=2,
    )
    own_normed, own_lse = partial_block(own_query, own_keys, own_values, allowed, factor)
    own_normed = (
        lax.optimization_barrier(own_normed)
        .astype(jnp.float32)
        .reshape(rows_local, heads_local, HD)
    )
    own_lse = own_lse.reshape(rows_local, heads_local)
    came_normed = lax.all_to_all(normed, "page", split_axis=0, concat_axis=0, tiled=True)
    came_lse = lax.all_to_all(lse, "page", split_axis=0, concat_axis=0, tiled=True)
    overall = jnp.maximum(jnp.max(came_lse, axis=0), own_lse)
    weights = jnp.exp(came_lse - overall[None])
    own_weight = jnp.exp(own_lse - overall)
    summed = (
        jnp.sum(came_normed.astype(jnp.float32) * weights[..., None], axis=0)
        + own_normed * own_weight[..., None]
    )
    denominator = jnp.sum(weights, axis=0) + own_weight
    attention = (summed / denominator[..., None]).astype(jnp.bfloat16).reshape(rows_local, width)
    all_rows = lax.all_gather(attention, "page", axis=0, tiled=True)
    return lax.psum_scatter(
        jnp.dot(all_rows, out_weight, preferred_element_type=jnp.float32),
        "tensor",
        scatter_dimension=0,
        tiled=True,
    ).astype(jnp.bfloat16)


def solution(mesh):
    placed = (
        P("page", None, "tensor"),
        P("page", "tensor"),
        P("page", "tensor"),
        P("page", "tensor"),
        P("page", "tensor"),
        P("page", None, "tensor"),
        P("page", None, "tensor"),
        P("page", None, "tensor"),
        P("page", None, "tensor"),
        P("page"),
        P(),
        P(),
        P("tensor", "page"),
    )
    return jax.shard_map(
        local, mesh=mesh, in_specs=placed, out_specs=P("tensor", "page"), check_vma=False
    )
```

profile of v0, /device:TPU:1, one launch (start us, length us, event | category | flops | bytes accessed | tf_op | source)
XLA Modules:
  0.0 326.2 jit_solution(7043587501592488716)
XLA Ops:
  6.5 0.7 all-gather.3.cloned.1.call-update
  7.3 0.7 broadcast_in_dim.84
  8.2 0.9 select_reduce_fusion
  9.1 1.3 maximum_bitcast_fusion
  10.4 88.8 %all-gather.3.cloned.1.call-done = bf16[128,4,1024]{2,1,0:T(4,128)(2,1)} async-done(((bf16[2,4,1024]{2,1,0:T(4,128)(2,1)}), bf16[128,4,1024]{2,1,0:T(4,128)(2,1)}) %all-gather.3.cloned.1.call-update) | async-done | bytes 1048592 | tf_op jit(solution)/shard_map/all_gather | solution.py:54
  99.2 1.5 reshape.210
  100.7 50.4 %while.13 = (s32[]{:T(128)}, bf16[8,1,64,1,8,128]{5,4,2,3,1,0:T(8,128)(2,1)}, f32[8,1,64,1,8]{4,2,3,1,0:T(8,128)S(1)}, s32[8]{0:T(128)S(1)}, s32[512]{0:T(512)S(...) while((s32[]{:T(128)}, ...), condition=%wide.region_4.5_spmd.clone, body=%wide.region_1.4_spmd.clone.sunk | while | flops 544407040 | bytes 14412756 | solution.py:82
  100.7 0.7 dynamic_slice.23
  103.8 1.1 fusion.62
  104.9 0.7 fusion.63
  105.6 1.4 fusion.64
  107.0 0.7 dynamic_slice.23
  110.1 1.1 fusion.62
  111.2 0.7 fusion.63
  111.9 1.4 fusion.64
  113.3 0.7 dynamic_slice.23
  116.4 1.1 fusion.62
  117.5 0.7 fusion.63
  118.2 1.4 fusion.64
  119.6 0.7 dynamic_slice.23
  122.7 1.1 fusion.62
  123.8 0.7 fusion.63
  124.5 1.4 fusion.64
  125.9 0.7 dynamic_slice.23
  129.0 1.1 fusion.62
  130.1 0.7 fusion.63
  130.8 1.4 fusion.64
  132.2 0.7 dynamic_slice.23
  135.3 1.1 fusion.62
  136.4 0.7 fusion.63
  137.1 1.4 fusion.64
  138.5 0.7 dynamic_slice.23
  141.5 1.1 fusion.62
  142.6 0.7 fusion.63
  143.3 1.4 fusion.64
  144.8 0.7 dynamic_slice.23
  147.8 1.1 fusion.62
  148.9 0.7 fusion.63
  149.6 1.4 fusion.64
  151.1 18.3 %all_to_all.10 = f32[64,8,8]{2,1,0:T(8,128)S(1)} all-to-all(f32[64,8,8]{2,1,0:T(8,128)S(1)} %bitcast.144), channel_id=1, replica_groups=mesh['page'=64,'tensor'=8] {'page'}, dimensions={0} | all-to-all | bytes 32768 | tf_op jit(solution)/shard_map/all_to_all | solution.py:110
  169.4 6.0 %all-to-all-start = ((bf16[64,8,8,128]{3,2,1,0:T(8,128)(2,1)}), bf16[64,8,8,128]{3,2,1,0:T(8,128)(2,1)S(1)}, u32[]{:S(2)}, u32[]{:S(2)}) async-start(bf16[64,8,8,128]{3,2,1,0:T(8,128)(2,1)} %bitcast.2), calls=%async_computation | async-start | bytes 2097152 | tf_op jit(solution)/shard_map/all_to_all | solution.py:109
  176.8 27.2 %all-to-all-done = bf16[64,8,8,128]{3,2,1,0:T(8,128)(2,1)S(1)} async-done(((bf16[64,8,8,128]{3,2,1,0:T(8,128)(2,1)}), bf16[64,8,8,128]{3,2,1,0:T(8,128)(2,1)S(1)}, u32[]{:S(2)}, u32[]{:S(2)}) %all-to-all-start) | async-done | bytes 1048608 | tf_op jit(solution)/shard_map/all_to_all | solution.py:109
  204.0 0.7 multiply_reduce_fusion
  204.7 0.7 fusion.44
  205.5 79.5 %all-gather.5.cloned.1.call-done = bf16[512,1024]{1,0:T(8,128)(2,1)} async-done(((bf16[8,1024]{1,0:T(8,128)(2,1)}), bf16[512,1024]{1,0:T(8,128)(2,1)}) %all-gather.5.cloned.1.call-update) | async-done | bytes 1048592 | tf_op jit(solution)/shard_map/all_gather | solution.py:120
  285.0 2.4 fusion.51
  287.4 30.9 %reduce-scatter.2.cloned.1.call-done = f32[64,80]{1,0:T(8,128)} async-done(((f32[512,80]{1,0:T(8,128)}), f32[64,80]{1,0:T(8,128)}) %reduce-scatter.2.cloned.1.call-update) | async-done | bytes 20496 | tf_op jit(solution)/shard_map/reduce_scatter | solution.py:121
  318.3 1.4 convert_element_type.34
  (89 shorter events, 3.8 us)
Async XLA Ops:
  6.5 278.5 %copy-start = (bf16[1024,80]{0,1:T(8,128)(2,1)S(1)}, bf16[1024,80]{0,1:T(8,128)(2,1)}, u32[]{:S(2)}) copy-start(bf16[1024,80]{0,1:T(8,128)(2,1)} %param.27) | copy-start | bytes 491524
  6.5 92.6 %all-gather.3.cloned.1.call-start = ((), (), s32[]{:S(2)}) async-start(), calls=%async_computation.3 | async-start | bytes 1064960 | tf_op jit(solution)/shard_map/all_gather | solution.py:54
  100.6 74.9 %copy-start.1 = (bf16[2,4,1024]{2,1,0:T(4,128)(2,1)S(1)}, bf16[2,4,1024]{2,1,0:T(4,128)(2,1)}, u32[]{:S(2)}) copy-start(bf16[2,4,1024]{2,1,0:T(4,128)(2,1)} %param.15) | copy-start | bytes 49156
  100.6 74.9 %copy-start.2 = (s32[2]{0:T(128)S(1)}, s32[2]{0:T(128)}, u32[]{:S(2)}) copy-start(s32[2]{0:T(128)} %param.24) | copy-start | bytes 28
  100.7 75.0 %copy-start.3 = (bf16[2,512,128]{2,1,0:T(8,128)(2,1)S(1)}, bf16[2,512,128]{2,1,0:T(8,128)(2,1)}, u32[]{:S(2)}) copy-start(bf16[2,512,128]{2,1,0:T(8,128)(2,1)} %param.20) | copy-start | bytes 786436
  100.7 75.0 %copy-start.5 = (bf16[2,4,128]{2,1,0:T(4,128)(2,1)S(1)}, bf16[2,4,128]{2,1,0:T(4,128)(2,1)}, u32[]{:S(2)}) copy-start(bf16[2,4,128]{2,1,0:T(4,128)(2,1)} %param.22) | copy-start | bytes 6148
  100.7 75.5 %copy-start.4 = (bf16[2,512,128]{2,1,0:T(8,128)(2,1)S(1)}, bf16[2,512,128]{2,1,0:T(8,128)(2,1)}, u32[]{:S(2)}) copy-start(bf16[2,512,128]{2,1,0:T(8,128)(2,1)} %param.21) | copy-start | bytes 786436
  100.7 75.5 %copy-start.6 = (bf16[2,4,128]{2,1,0:T(4,128)(2,1)S(1)}, bf16[2,4,128]{2,1,0:T(4,128)(2,1)}, u32[]{:S(2)}) copy-start(bf16[2,4,128]{2,1,0:T(4,128)(2,1)} %param.23) | copy-start | bytes 6148
  169.4 34.6 %all-to-all-start = ((bf16[64,8,8,128]{3,2,1,0:T(8,128)(2,1)}), bf16[64,8,8,128]{3,2,1,0:T(8,128)(2,1)S(1)}, u32[]{:S(2)}, u32[]{:S(2)}) async-start(bf16[64,8,8,128]{3,2,1,0:T(8,128)(2,1)} %bitcast.2), calls=%async_computation | async-start | bytes 2097152 | tf_op jit(solution)/shard_map/all_to_all | solution.py:109
  175.5 109.5 %all-gather.5.cloned.1.call-start = ((), (), s32[]{:S(2)}) async-start(), calls=%async_computation.4 | async-start | bytes 1064960 | tf_op jit(solution)/shard_map/all_gather | solution.py:120
  205.4 112.9 %reduce-scatter.2.cloned.1.call-start = ((), (), s32[]{:S(2)}) async-start(), calls=%async_computation.5 | async-start | bytes 294912 | tf_op jit(solution)/shard_map/reduce_scatter | solution.py:121
Sparse Core Ops, SparseCore 0:
  10.7 88.3 all-gather.2
  205.6 79.3 all-gather.4
  287.8 30.4 reduce-scatter.1
where the time goes:
time: 331 us; the launch traced here: 326 us
  waiting for transfers between devices  227 us (69%)
  matrix products  23.1 us (7%)
  blocking collectives  18.3 us (6%)
  loops' own time  16.9 us (5%)
  between operations  13.3 us (4%)
  other arithmetic  12 us (4%)
  local copies, waits for them, and re-layouts  9.23 us (3%)
  starting transfers between devices  6.11 us (2%)
    all_gather x1, waiting for transfers between devices, local(): gathered = lax.all_gather(queries, 'page', axis=0, tiled=True)  88.8 us
    all_gather x1, waiting for transfers between devices, local(): all_rows = lax.all_gather(attention, 'page', axis=0, tiled=True)  79.5 us
    reduce_scatter x1, waiting for transfers between devices, local(): lax.psum_scatter(jnp.dot(all_rows, out_weight, preferred_element_type=jnp...  30.9 us
    all_to_all x1, waiting for transfers between devices, local(): lax.all_to_all(normed, 'page', split_axis=0, concat_axis=0, tiled=True)  27.2 us
    all_to_all x1, blocking collectives, local(): lax.all_to_all(lse, 'page', split_axis=0, concat_axis=0, tiled=True)  18.3 us
    another operation x1, loops' own time, local(): lax.map(one_block, jnp.arange(rows_all // block_rows) * block_rows)  16.9 us
    dot_general x9, matrix products, partial_block(): jnp.einsum('bskgn,bnkd->bskgd', powers.astype(jnp.bfloat16), value_rows,...  11.6 us
    dot_general x9, matrix products, partial_block(): jnp.einsum('bskgd,bnkd->bskgn', query_rows, key_rows, preferred_element_t...  9.1 us
  transfers between devices with their start and end apart: 4, of which 4 were waited for; matrix products, arithmetic and copies ran while one was open for 1% of the time, Pallas kernels for 0%

commit v1 on v0

v1 whole, which is shorter than its diff:
```python
import functools
import math

import jax
import jax.numpy as jnp
from jax import lax
from jax.experimental import pallas as pl
from jax.experimental.pallas import tpu as pltpu
from jax.sharding import PartitionSpec as P

HD = 128
PAGE = 256
HEADS = 8
X, Z = 4, 8
CHIPS = X * Z
T = 8
ROWS = CHIPS * 8
WIDTH = HEADS * HD
PACKED = WIDTH + 128
FACTOR = 1.0 / math.sqrt(HD)
LOG2E = math.log2(math.e)
NEG = -1e30
NT = (((1,), (1,)), ((), ()))
BF16, F32 = jnp.bfloat16, jnp.float32
VMEM = pl.BlockSpec(memory_space=pltpu.VMEM)
SMEM = pl.BlockSpec(memory_space=pltpu.SMEM)


def page_id(x, z, core):
    return (x * Z + z) * 2 + core


XZ_GROUPS = [[page_id(x, z, c) for x in range(X) for z in range(Z)] for c in range(2)]
X_GROUPS = [[page_id(x, z, c) for x in range(X)] for z in range(Z) for c in range(2)]
ZT_GROUPS = [
    [page_id(x, z, c) * T + t for z in range(Z) for t in range(T)] for x in range(X) for c in range(2)
]
CORE_SWAP = [(p, p ^ 1) for p in range(2 * CHIPS)]


def split3(x):
    high = x.astype(BF16).astype(F32)
    rest = x - high
    middle = rest.astype(BF16).astype(F32)
    return high, middle, rest - middle


def attend_kernel(
    chip_ref, groups_ref, q_ref, row_group_ref, own_ref, own_lse_ref, pk_ref, pv_ref, gk_ref, gv_ref, other_ref,
    out_ref, q_rows, own_rows,
):
    source = lambda n, k: (lax.broadcasted_iota(jnp.int32, (n, k), 0) % 8) * CHIPS + (
        lax.broadcasted_iota(jnp.int32, (n, k), 0) // 8
    )
    order = (source(ROWS, ROWS) == lax.broadcasted_iota(jnp.int32, (ROWS, ROWS), 1)).astype(BF16)
    q_rows[...] = jnp.dot(order, q_ref[...], preferred_element_type=F32).astype(BF16)
    first = chip_ref[0] * 8
    place = (source(ROWS, 8) == lax.broadcasted_iota(jnp.int32, (ROWS, 8), 1) + first).astype(BF16)
    own_rows[:, :WIDTH] = jnp.dot(place, own_ref[...], preferred_element_type=F32)
    own_lse = functools.reduce(
        jnp.add,
        [jnp.dot(place, part.astype(BF16), preferred_element_type=F32) for part in split3(own_lse_ref[...])],
    )
    at = source(ROWS, 128)
    own_rows[:, WIDTH:] = jnp.where((at >= first) & (at < first + 8), own_lse, NEG)
    lane = lax.broadcasted_iota(jnp.int32, (ROWS, 128), 1)
    row_group = row_group_ref[...]
    bias = [jnp.where(row_group == groups_ref[j], 0.0, NEG) for j in range(8)]
    stats = jnp.zeros((ROWS, 128), F32)
    for h in range(HEADS):
        cols = slice(h * HD, (h + 1) * HD)
        q = q_rows[:, cols]
        keys = [pk_ref[...], other_ref[0:1024, :], gk_ref[...], other_ref[1024:2048, :]]
        values = [pv_ref[...], other_ref[2048:3072, :], gv_ref[...], other_ref[3072:4096, :]]
        scores = [lax.dot_general(q, k, NT, preferred_element_type=F32) for k in keys]
        for b in (0, 1):
            scores[2 + b] = jnp.concatenate(
                [scores[2 + b][:, j * PAGE : (j + 1) * PAGE] + bias[4 * b + j] for j in range(4)], axis=1
            )
        peak = functools.reduce(jnp.maximum, [jnp.max(s, axis=1, keepdims=True) for s in scores])
        peak = peak * (FACTOR * LOG2E)
        mass, total = 0.0, 0.0
        for s, v in zip(scores, values):
            power = jnp.exp2(s * (FACTOR * LOG2E) - peak)
            mass = mass + jnp.sum(power, axis=1, keepdims=True)
            total = total + jnp.dot(power.astype(BF16), v, preferred_element_type=F32)
        own_l = own_rows[:, WIDTH + h : WIDTH + h + 1]
        top = jnp.maximum(peak, own_l)
        scale, own_scale = jnp.exp2(peak - top), jnp.exp2(own_l - top)
        mass = mass * scale + own_scale
        total = total * scale + own_rows[:, cols] * own_scale
        out_ref[:, cols] = (total / mass).astype(BF16)
        high, middle, low = split3(top + jnp.log2(mass))
        stats = jnp.where(
            lane == h, high, jnp.where(lane == 8 + h, middle, jnp.where(lane == 16 + h, low, stats))
        )
    out_ref[:, WIDTH:] = stats.astype(BF16)


def merge_kernel(came_ref, out_ref, rows_ref):
    parts = came_ref[:, :, WIDTH:].astype(F32)
    lse = parts + pltpu.roll(parts, 120, 2) + pltpu.roll(parts, 112, 2)
    top = jnp.max(lse, axis=0, keepdims=True)
    weights = jnp.exp2(lse - top)
    weights = weights / jnp.sum(weights, axis=0, keepdims=True)
    for h in range(HEADS):
        rows = came_ref[:, :, h * HD : (h + 1) * HD].astype(F32)
        rows_ref[:, h, :] = jnp.sum(rows * weights[:, :, h : h + 1], axis=0)
    rows = rows_ref[...].astype(BF16)
    for z in range(Z):
        out_ref[z] = rows


def own_partial(queries, suffix_keys, suffix_values, new_keys, new_values, suffix_lengths):
    owned, steps, _ = queries.shape
    suffix_len = suffix_keys.shape[1]
    own_query = queries.reshape(owned, steps, HEADS, HD)
    own_keys = jnp.concatenate([suffix_keys, new_keys], axis=1)
    own_values = jnp.concatenate([suffix_values, new_values], axis=1)
    old_allowed = jnp.arange(suffix_len)[None, None, :] < suffix_lengths[:, None, None]
    new_allowed = jnp.arange(steps)[None, :, None] >= jnp.arange(steps)[None, None, :]
    allowed = jnp.concatenate(
        [
            jnp.broadcast_to(old_allowed, (owned, steps, suffix_len)),
            jnp.broadcast_to(new_allowed, (owned, steps, steps)),
        ],
        axis=2,
    )
    scores = jnp.einsum("bshd,bnd->bshn", own_query, own_keys, preferred_element_type=F32) * (FACTOR * LOG2E)
    scores = jnp.where(allowed[:, :, None, :], scores, -jnp.inf)
    maxima = jnp.max(scores, axis=-1)
    powers = jnp.exp2(scores - maxima[..., None])
    totals = jnp.sum(powers, axis=-1)
    outputs = jnp.einsum("bshn,bnd->bshd", powers.astype(BF16), own_values, preferred_element_type=F32)
    normed = (outputs / totals[..., None]).astype(BF16).reshape(owned * steps, WIDTH)
    lse = (maxima + jnp.log2(totals)).reshape(owned * steps, HEADS)
    return normed, jnp.pad(lse, ((0, 0), (0, 128 - HEADS)))


def local(
    queries,
    prompt_keys,
    prompt_values,
    pool_keys,
    pool_values,
    suffix_keys,
    suffix_values,
    new_keys,
    new_values,
    suffix_lengths,
    branch_group,
    page_list,
    out_weight,
):
    page = lax.axis_index("page")
    core, chip = page % 2, page // 2
    sent = jnp.broadcast_to(queries.reshape(1, 8, WIDTH), (CHIPS, 8, WIDTH))
    gathered = lax.all_to_all(sent, "page", 0, 0, tiled=True, axis_index_groups=XZ_GROUPS)
    gathered = gathered.reshape(ROWS, WIDTH)
    other = jnp.concatenate([prompt_keys, pool_keys, prompt_values, pool_values], axis=0)
    other = lax.ppermute(other, "page", CORE_SWAP)
    weight = lax.all_gather(out_weight, "tensor", axis=0, tiled=True)

    row_group = jnp.repeat(branch_group, 4).reshape(T, X, 2, Z)
    row_group = lax.dynamic_index_in_dim(row_group, core, 2, keepdims=False)
    row_group = row_group.transpose(1, 2, 0).reshape(ROWS, 1)
    page_ids = jnp.concatenate([page * 4 + jnp.arange(4), (page ^ 1) * 4 + jnp.arange(4)])
    matched = page_list[:, :, None] == page_ids[None, None, :]
    page_group = jnp.sum(
        jnp.where(matched, jnp.arange(page_list.shape[0])[:, None, None], 0), axis=(0, 1)
    )
    own, own_lse = own_partial(
        queries, suffix_keys, suffix_values, new_keys, new_values, suffix_lengths
    )
    packed = pl.pallas_call(
        attend_kernel,
        out_shape=jax.ShapeDtypeStruct((ROWS, PACKED), BF16),
        in_specs=[SMEM, SMEM] + [VMEM] * 9,
        out_specs=VMEM,
        scratch_shapes=[pltpu.VMEM((ROWS, WIDTH), BF16), pltpu.VMEM((ROWS, PACKED), F32)],
        compiler_params=pltpu.CompilerParams(vmem_limit_bytes=48 * 1024 * 1024),
    )(
        chip.reshape(1), page_group, gathered, row_group, own, own_lse,
        prompt_keys, prompt_values, pool_keys, pool_values, other,
    )
    came = lax.all_to_all(
        packed.reshape(CHIPS, 8, PACKED), "page", 0, 0, tiled=True, axis_index_groups=XZ_GROUPS
    )
    rows = pl.pallas_call(
        merge_kernel,
        out_shape=jax.ShapeDtypeStruct((Z, T, HEADS, HD), BF16),
        in_specs=[VMEM],
        out_specs=VMEM,
        scratch_shapes=[pltpu.VMEM((8, HEADS, HD), F32)],
    )(came)
    rows = lax.all_to_all(
        rows.reshape(Z * T, HEADS, HD), ("page", "tensor"), 0, 0, tiled=True, axis_index_groups=ZT_GROUPS
    )
    rows = jnp.broadcast_to(rows.reshape(1, Z, T * WIDTH), (X, Z, T * WIDTH))
    rows = lax.all_to_all(rows, "page", 0, 0, tiled=True, axis_index_groups=X_GROUPS)
    rows = rows.reshape(CHIPS, T * WIDTH)
    rows_other = lax.ppermute(rows, "page", CORE_SWAP)
    mine = jnp.dot(rows, weight, preferred_element_type=F32).astype(BF16).reshape(X, 1, Z, -1)
    theirs = jnp.dot(rows_other, weight, preferred_element_type=F32).astype(BF16).reshape(X, 1, Z, -1)
    both = jnp.where(
        core == 0, jnp.concatenate([mine, theirs], axis=1), jnp.concatenate([theirs, mine], axis=1)
    )
    return both.reshape(2 * CHIPS, -1)


def solution(mesh):
    placed = (
        P("page", None, "tensor"),
        P("page", "tensor"),
        P("page", "tensor"),
        P("page", "tensor"),
        P("page", "tensor"),
        P("page", None, "tensor"),
        P("page", None, "tensor"),
        P("page", None, "tensor"),
        P("page", None, "tensor"),
        P("page"),
        P(),
        P(),
        P("tensor", "page"),
    )
    return jax.shard_map(
        local, mesh=mesh, in_specs=placed, out_specs=P("tensor", "page"), check_vma=False
    )
```

time: 331 us -> 131 us (0.40); the launches traced: 326 us -> 131 us
  waiting for transfers between devices: 227 us -> 13.1 us
  blocking collectives: 18.3 us -> 56.1 us
  matrix products: 23.1 us -> 2.9 us
  Pallas kernels: 0 us -> 17.5 us
  loops' own time: 16.9 us -> 0 us
  starting transfers between devices: 6.11 us -> 22.8 us
  other arithmetic: 12 us -> 2.81 us
  local copies, waits for them, and re-layouts: 9.23 us -> 2.09 us
    all_gather x2 -> x1, waiting for transfers between devices: 168 us -> 0.02 us  [local(): weight = lax.all_gather(out_weight, 'tensor', axis=0, tiled=True)]
    all_to_all x1 -> x3, blocking collectives: 18.3 us -> 56.1 us  [the longest x1 23.1 us: local(): lax.all_to_all(rows.reshape(Z * T, HEADS, HD), ('page', 'tensor'), 0, 0,...]
    reduce_scatter x1 -> x0, waiting for transfers between devices: 30.9 us -> none  [local(): lax.psum_scatter(jnp.dot(all_rows, out_weight, preferred_element_type=jnp...]
    dot_general x19 -> x4, matrix products: 23.1 us -> 2.9 us  [the longest x1 1.89 us: local(): jnp.dot(rows, weight, preferred_element_type=F32).astype(BF16)]
    pallas_call x0 -> x2, Pallas kernels: none -> 17.5 us  [the longest x1 15.2 us: local(): pl.pallas_call(attend_kernel, out_shape=jax.ShapeDtypeStruct((ROWS, PACKE...]
    another operation x1 -> x0, loops' own time: 16.9 us -> none  [local(): lax.map(one_block, jnp.arange(rows_all // block_rows) * block_rows)]
    ppermute x0 -> x2, starting transfers between devices: none -> 15.1 us  [the longest x1 8.92 us: local(): other = lax.ppermute(other, 'page', CORE_SWAP)]
    all_to_all x1, waiting for transfers between devices: 27.2 us -> 12.4 us  [local(): lax.all_to_all(sent, 'page', 0, 0, tiled=True, axis_index_groups=XZ_GROUPS)]
  transfers between devices with their start and end apart: 4 -> 4, of which waited for: 4 -> 1; matrix products, arithmetic and copies ran while one was open for 1% -> 3% of each run, Pallas kernels for 0% -> 13%
where the time goes in v1:
time: 131 us
  blocking collectives  56.1 us (43%)
  starting transfers between devices  22.8 us (17%)
  Pallas kernels  17.5 us (13%)
  between operations  13.7 us (10%)
  waiting for transfers between devices  13.1 us (10%)
  matrix products  2.9 us (2%)
  other arithmetic  2.81 us (2%)
  local copies, waits for them, and re-layouts  2.09 us (2%)
    all_to_all x1, blocking collectives, local(): lax.all_to_all(rows.reshape(Z * T, HEADS, HD), ('page', 'tensor'), 0, 0,...  23.1 us
    all_to_all x1, blocking collectives, local(): lax.all_to_all(packed.reshape(CHIPS, 8, PACKED), 'page', 0, 0, tiled=True...  23 us
    pallas_call x1, Pallas kernels, local(): pl.pallas_call(attend_kernel, out_shape=jax.ShapeDtypeStruct((ROWS, PACKE...  15.2 us
    all_to_all x1, waiting for transfers between devices, local(): lax.all_to_all(sent, 'page', 0, 0, tiled=True, axis_index_groups=XZ_GROUPS)  12.4 us
    all_to_all x1, blocking collectives, local(): lax.all_to_all(rows, 'page', 0, 0, tiled=True, axis_index_groups=X_GROUPS)  10.1 us
    ppermute x1, starting transfers between devices, local(): other = lax.ppermute(other, 'page', CORE_SWAP)  8.92 us
    all_to_all x1, starting transfers between devices, local(): lax.all_to_all(sent, 'page', 0, 0, tiled=True, axis_index_groups=XZ_GROUPS)  7.64 us
    ppermute x1, starting transfers between devices, local(): rows_other = lax.ppermute(rows, 'page', CORE_SWAP)  6.19 us
  transfers between devices with their start and end apart: 4, of which 1 were waited for; matrix products, arithmetic and copies ran while one was open for 3% of the time, Pallas kernels for 13%

profile of v1, /device:TPU:1, one launch (start us, length us, event | category | flops | bytes accessed | tf_op | source)
XLA Modules:
  0.0 131.0 jit_solution(17982374194829217992)
XLA Ops:
  6.5 2.2 %pad_maximum_fusion = bf16[4096,128]{1,0:T(8,128)(2,1)} fusion(bf16[1024,128]{1,0:T(8,128)(2,1)} %gv_ref.1, bf16[1024,128]{1,0:T(8,128)(2,1)} %pv_ref.1, bf16[1024,128]{1,0:T(8,128)(2,1)} %gk_ref.1, bf16[1024,128]{1,0:T(8,128)(2,1)} %pk_ref.1), kind=kLoop, calls=%fused_computation.9 | loop fusion | flops 4194304 | bytes 2097152 | tf_op jit(solution)/shard_map/concatenate | solution.py:160
  8.8 8.9 %collective-permute-start = (bf16[4096,128]{1,0:T(8,128)(2,1)}, bf16[4096,128]{1,0:T(8,128)(2,1)S(1)}, u32[]{:S(2)}, u32[]{:S(2)}) collective-permute-start(bf16[4096,128]{1,0:T(8,128)(2,1)} %pad_maximum_fusion), channel_id=1, source_target_pairs={{0,8},{8,0},{16,24},{24,16},{32,40},{40,32},{48,56},{56,48},{64,72... | collective-permute-start | bytes 3145736 | tf_op jit(solution)/shard_map/ppermute | solution.py:161
  17.7 0.0 copy-done.5
  17.7 0.9 broadcast_in_dim.68
  18.6 7.6 %all-to-all-start = ((bf16[32,8,1024]{2,1,0:T(8,128)(2,1)}), bf16[32,8,1024]{2,1,0:T(8,128)(2,1)S(1)}, u32[]{:S(2)}, u32[]{:S(2)}) async-start(bf16[32,8,1024]{2,1,0:T(8,128)(2,1)} %broadcast_in_dim.68), calls=%async_computation | async-start | bytes 1048576 | tf_op jit(solution)/shard_map/all_to_all | solution.py:158
  26.2 0.0 copy-start.6
  26.3 0.0 copy-start
  26.3 0.0 copy-start.1
  26.3 0.0 copy-start.2
  26.3 0.0 copy-start.3
  26.3 0.0 all-gather.2.cloned.1.call-start
  26.4 0.7 all-gather.2.cloned.1.call-update
  27.1 0.0 copy-done.8
  27.1 0.1 iota_compare_fusion
  27.2 0.0 copy-done.9
  27.2 0.0 copy-done.11
  27.2 0.3 fusion.18
  27.5 0.0 copy-done.7
  27.5 0.2 broadcast_in_dim.69
  27.7 0.1 copy.19
  27.8 0.1 reshape.101.row_group_ref
  28.0 0.2 fusion.9
  28.1 0.0 copy-done.10
  28.1 0.0 copy-done.12
  28.2 0.2 fusion.2
  28.5 0.1 pad_add_fusion.1
  28.5 0.0 copy-done.6
  28.5 0.2 select_reduce_fusion.groups_ref
  28.7 12.4 %all-to-all-done = bf16[32,8,1024]{2,1,0:T(8,128)(2,1)S(1)} async-done(((bf16[32,8,1024]{2,1,0:T(8,128)(2,1)}), bf16[32,8,1024]{2,1,0:T(8,128)(2,1)S(1)}, u32[]{:S(2)}, u32[]{:S(2)}) %all-to-all-start) | async-done | bytes 524320 | tf_op jit(solution)/shard_map/all_to_all | solution.py:158
  41.1 0.0 collective-permute-done.other_ref
  41.1 0.0 copy-done
  41.1 0.0 copy-done.1
  41.1 0.0 copy-done.2
  41.1 0.0 copy-done.3
  41.1 15.2 %shard_map.127 = bf16[256,1152]{1,0:T(8,128)(2,1)S(1)} custom-call(s32[1]{0:T(128)} %bitcast.chip_ref, s32[8]{0:T(128)S(1)} %select_reduce_fusion.groups_ref, bf16[256,1024]{1,0:T(8,128)(2,1)S(1)} %bitcast.44, s32[256,1]{1,0:T(8,128)S(1)} %reshape.101.row_group_ref, bf16[8,1024]{1,0:T(8,128)(2,1)S(1)} %bitcast.45, f32[8,128]{1,0:T(8,128)S(1)} %pad.4.own_lse_ref, ...), custom_call_target="tpu_custom_call" | custom-call | tf_op jit(solution)/shard_map/pallas_call | solution.py:175
  56.4 23.0 %all_to_all.20.came_ref = bf16[32,8,1152]{2,1,0:T(8,128)(2,1)} all-to-all(bf16[32,8,1152]{2,1,0:T(8,128)(2,1)S(1)} %bitcast.43), channel_id=1, replica_groups={{0,16,32,48,64,80,96,112,128,144,160,176,192,208,224,240,256,272,288,30..., dimensions={0} | all-to-all | bytes 1179648 | tf_op jit(solution)/shard_map/all_to_all | solution.py:186
  79.3 2.2 %shard_map.128 = bf16[8,8,8,128]{3,2,1,0:T(8,128)(2,1)} custom-call(bf16[32,8,1152]{2,1,0:T(8,128)(2,1)} %all_to_all.20.came_ref), custom_call_target="tpu_custom_call" | custom-call | tf_op jit(solution)/shard_map/pallas_call | solution.py:189
  81.6 23.1 %all_to_all.21 = bf16[64,8,128]{2,1,0:T(8,128)(2,1)S(1)} all-to-all(bf16[64,8,128]{2,1,0:T(8,128)(2,1)} %bitcast.47), channel_id=1, replica_groups={{0,1,2,3,4,5,6,7,16,17,18,19,20,21,22,23,32,33,34,35,36,37,38,39,48,49,..., dimensions={0} | all-to-all | bytes 262144 | tf_op jit(solution)/shard_map/all_to_all | solution.py:196
  104.6 0.1 broadcast_in_dim.76
  104.8 10.1 %all_to_all.22 = bf16[4,8,8192]{2,1,0:T(8,128)(2,1)S(1)} all-to-all(bf16[4,8,8192]{2,1,0:T(8,128)(2,1)S(1)} %broadcast_in_dim.77), channel_id=1, replica_groups={{0,128,256,384},{8,136,264,392},{16,144,272,400},{24,152,280,408},{32,1..., dimensions={0} | all-to-all | bytes 1048576 | tf_op jit(solution)/shard_map/all_to_all | solution.py:200
  114.9 6.2 %collective-permute-start.1 = (bf16[32,8192]{1,0:T(8,128)(2,1)S(1)}, bf16[32,8192]{1,0:T(8,128)(2,1)S(1)}, u32[]{:S(2)}, u32[]{:S(2)}) collective-permute-start(bf16[32,8192]{1,0:T(8,128)(2,1)S(1)} %bitcast.46), channel_id=1, source_target_pairs={{0,8},{8,0},{16,24},{24,16},{32,40},{40,32},{48,56},{56,48},{64,72... | collective-permute-start | bytes 1572872 | tf_op jit(solution)/shard_map/ppermute | solution.py:202
  121.1 0.0 all-gather.2.cloned.1.call-done
  121.1 0.0 copy-start.4
  121.1 1.9 %fusion.3 = bf16[4,1,8,80]{3,2,0,1:T(8,128)(2,1)S(1)} fusion(bf16[8192,80]{0,1:T(8,128)(2,1)} %all-gather.2.cloned.1.call-done, bf16[4,8,8192]{2,1,0:T(8,128)(2,1)S(1)} %all_to_all.22), kind=kOutput, calls=%fused_computation.7 | convolution fusion | flops 41945600 | bytes 1840128 | tf_op jit(solution)/shard_map/dot_general | solution.py:203
  123.0 0.0 collective-permute-done.1
  123.0 0.0 copy-done.4
  123.0 0.5 fusion.4
  123.5 0.6 copy.21
  (21 shorter events, 0.2 us)
Async XLA Ops:
  6.5 11.2 %copy-start.5 = (bf16[2,4,1024]{2,1,0:T(4,128)(2,1)S(1)}, bf16[2,4,1024]{2,1,0:T(4,128)(2,1)}, u32[]{:S(2)}) copy-start(bf16[2,4,1024]{2,1,0:T(4,128)(2,1)} %param.13) | copy-start | bytes 49156
  8.8 18.3 %copy-start.8 = (s32[2]{0:T(128)S(1)}, s32[2]{0:T(128)}, u32[]{:S(2)}) copy-start(s32[2]{0:T(128)} %param.22) | copy-start | bytes 28
  8.8 18.4 %copy-start.9 = (bf16[2,512,128]{2,1,0:T(8,128)(2,1)S(1)}, bf16[2,512,128]{2,1,0:T(8,128)(2,1)}, u32[]{:S(2)}) copy-start(bf16[2,512,128]{2,1,0:T(8,128)(2,1)} %param.18) | copy-start | bytes 786436
  8.8 18.5 %copy-start.11 = (bf16[2,4,128]{2,1,0:T(4,128)(2,1)S(1)}, bf16[2,4,128]{2,1,0:T(4,128)(2,1)}, u32[]{:S(2)}) copy-start(bf16[2,4,128]{2,1,0:T(4,128)(2,1)} %param.20) | copy-start | bytes 6148
  8.8 18.7 %copy-start.7 = (s32[128]{0:T(128)S(1)}, s32[128]{0:T(128)}, u32[]{:S(2)}) copy-start(s32[128]{0:T(128)} %param.23) | copy-start | bytes 1540
  8.8 32.3 %collective-permute-start = (bf16[4096,128]{1,0:T(8,128)(2,1)}, bf16[4096,128]{1,0:T(8,128)(2,1)S(1)}, u32[]{:S(2)}, u32[]{:S(2)}) collective-permute-start(bf16[4096,128]{1,0:T(8,128)(2,1)} %pad_maximum_fusion), channel_id=1, source_target_pairs={{0,8},{8,0},{16,24},{24,16},{32,40},{40,32},{48,56},{56,48},{64,72... | collective-permute-start | bytes 3145736 | tf_op jit(solution)/shard_map/ppermute | solution.py:161
  18.6 9.5 %copy-start.10 = (bf16[2,512,128]{2,1,0:T(8,128)(2,1)S(1)}, bf16[2,512,128]{2,1,0:T(8,128)(2,1)}, u32[]{:S(2)}) copy-start(bf16[2,512,128]{2,1,0:T(8,128)(2,1)} %param.19) | copy-start | bytes 786436
  18.6 9.6 %copy-start.12 = (bf16[2,4,128]{2,1,0:T(4,128)(2,1)S(1)}, bf16[2,4,128]{2,1,0:T(4,128)(2,1)}, u32[]{:S(2)}) copy-start(bf16[2,4,128]{2,1,0:T(4,128)(2,1)} %param.21) | copy-start | bytes 6148
  18.6 22.5 %all-to-all-start = ((bf16[32,8,1024]{2,1,0:T(8,128)(2,1)}), bf16[32,8,1024]{2,1,0:T(8,128)(2,1)S(1)}, u32[]{:S(2)}, u32[]{:S(2)}) async-start(bf16[32,8,1024]{2,1,0:T(8,128)(2,1)} %broadcast_in_dim.68), calls=%async_computation | async-start | bytes 1048576 | tf_op jit(solution)/shard_map/all_to_all | solution.py:158
  26.2 2.3 %copy-start.6 = (s32[16,16]{1,0:T(8,128)S(1)}, s32[16,16]{1,0:T(8,128)}, u32[]{:S(2)}) copy-start(s32[16,16]{1,0:T(8,128)} %param.24) | copy-start | bytes 3076
  26.3 14.9 %copy-start = (bf16[1024,128]{1,0:T(8,128)(2,1)S(1)}, bf16[1024,128]{1,0:T(8,128)(2,1)}, u32[]{:S(2)}) copy-start(bf16[1024,128]{1,0:T(8,128)(2,1)} %pk_ref.1) | copy-start | bytes 786436
  26.3 14.8 %copy-start.1 = (bf16[1024,128]{1,0:T(8,128)(2,1)S(1)}, bf16[1024,128]{1,0:T(8,128)(2,1)}, u32[]{:S(2)}) copy-start(bf16[1024,128]{1,0:T(8,128)(2,1)} %pv_ref.1) | copy-start | bytes 786436
  26.3 14.8 %copy-start.2 = (bf16[1024,128]{1,0:T(8,128)(2,1)S(1)}, bf16[1024,128]{1,0:T(8,128)(2,1)}, u32[]{:S(2)}) copy-start(bf16[1024,128]{1,0:T(8,128)(2,1)} %gk_ref.1) | copy-start | bytes 786436
  26.3 14.8 %copy-start.3 = (bf16[1024,128]{1,0:T(8,128)(2,1)S(1)}, bf16[1024,128]{1,0:T(8,128)(2,1)}, u32[]{:S(2)}) copy-start(bf16[1024,128]{1,0:T(8,128)(2,1)} %gv_ref.1) | copy-start | bytes 786436
  26.3 94.8 %all-gather.2.cloned.1.call-start = ((), (), s32[]{:S(2)}) async-start(), calls=%async_computation.4 | async-start | bytes 1474560 | tf_op jit(solution)/shard_map/all_gather | solution.py:162
  114.9 8.2 %collective-permute-start.1 = (bf16[32,8192]{1,0:T(8,128)(2,1)S(1)}, bf16[32,8192]{1,0:T(8,128)(2,1)S(1)}, u32[]{:S(2)}, u32[]{:S(2)}) collective-permute-start(bf16[32,8192]{1,0:T(8,128)(2,1)S(1)} %bitcast.46), channel_id=1, source_target_pairs={{0,8},{8,0},{16,24},{24,16},{32,40},{40,32},{48,56},{56,48},{64,72... | collective-permute-start | bytes 1572872 | tf_op jit(solution)/shard_map/ppermute | solution.py:202
  121.1 1.9 %copy-start.4 = (bf16[8192,80]{0,1:T(8,128)(2,1)S(1)}, bf16[8192,80]{0,1:T(8,128)(2,1)}, u32[]{:S(2)}) copy-start(bf16[8192,80]{0,1:T(8,128)(2,1)} %all-gather.2.cloned.1.call-done) | copy-start | bytes 3932164
Sparse Core Ops, SparseCore 0:
  29.2 38.4 all-gather.1

commit v2 on v1

v2 whole, which is shorter than its diff:
```python
import functools
import math

import jax
import jax.numpy as jnp
from jax import lax
from jax.experimental import pallas as pl
from jax.experimental.pallas import tpu as pltpu
from jax.sharding import PartitionSpec as P

HD = 128
PAGE = 256
HEADS = 8
X, Z = 4, 8
CHIPS = X * Z
T = 8
ROWS = CHIPS * 8
WIDTH = HEADS * HD
PACKED = WIDTH + 128
SUFFIX = 512
SCALE = math.log2(math.e) / math.sqrt(HD)
PROMPT, KEYS = 2048, 4096
WINDOW = 64
OFFSETS = (0, 4, 2, 6, 1, 5, 7, 3)
WEIGHT_AT = ((0, 0), (0, 1), (1, 0), (2, 0), (3, 0), (3, 1), (4, 0), (4, 1))
NEG = -1e30
NT = (((1,), (1,)), ((), ()))
BF16, F32 = jnp.bfloat16, jnp.float32
VMEM = pl.BlockSpec(memory_space=pltpu.VMEM)
SMEM = pl.BlockSpec(memory_space=pltpu.SMEM)
HBM = pl.BlockSpec(memory_space=pltpu.HBM)
PARAMS = pltpu.CompilerParams(vmem_limit_bytes=60 * 1024 * 1024)
SMALL = pltpu.CompilerParams(vmem_limit_bytes=8 * 1024 * 1024)


def page_id(x, z, core):
    return (x * Z + z) * 2 + core


XZ_GROUPS = [[page_id(x, z, c) for x in range(X) for z in range(Z)] for c in range(2)]
X_GROUPS = [[page_id(x, z, c) for x in range(X)] for z in range(Z) for c in range(2)]
ZT_GROUPS = [
    [page_id(x, z, c) * T + t for z in range(Z) for t in range(T)] for x in range(X) for c in range(2)
]
CORE_SWAP = [(p, p ^ 1) for p in range(2 * CHIPS)]


def split3(x):
    high = x.astype(BF16).astype(F32)
    rest = x - high
    middle = rest.astype(BF16).astype(F32)
    return high, middle, rest - middle


def spread_kernel(q_ref, out_ref):
    rows = jnp.concatenate([q_ref[0].astype(F32), q_ref[1].astype(F32)], axis=0).astype(BF16)
    for i in range(CHIPS):
        out_ref[i] = rows


def copies_of(pairs, sems):
    return [pltpu.make_async_copy(a, b, sems.at[i]) for i, (a, b) in enumerate(pairs)]


def prep_kernel(
    chip_ref, groups_ref, lengths_ref, row_group_ref, new_keys_ref, new_values_ref, *refs,
):
    sources, results, held, made = refs[:7], refs[7:15], refs[15:25], refs[25:33]
    in_sems, out_sems = refs[33:]
    sources = sources[:4] + tuple(sources[4].at[n * 1024 : (n + 1) * 1024] for n in range(4)) + sources[5:]
    suffix_keys_ref, suffix_values_ref = held[8:]
    keys_ref, values_ref, own_keys_ref, own_values_ref, longest_ref, sort_ref, unsort_ref, marks_ref = made
    incoming = copies_of(list(zip(sources, held)), in_sems)
    quarters = [slice(n * 1024, (n + 1) * 1024) for n in range(4)]
    outgoing = copies_of(
        list(zip(made[2:], results[2:]))
        + [(made[i].at[rows], results[i].at[rows]) for rows in quarters for i in (0, 1)],
        out_sems,
    )
    for copy in incoming:
        copy.start()
    lane = lax.broadcasted_iota(jnp.int32, (PAGE, 128), 1)
    ones = jnp.ones((PAGE, HD), BF16)
    down = lax.broadcasted_iota(jnp.int32, (ROWS, ROWS), 0)
    across = lax.broadcasted_iota(jnp.int32, (ROWS, ROWS), 1)
    group_across = row_group_ref[...]
    group_down = jnp.sum(jnp.where(down == across, group_across, 0), axis=1, keepdims=True)
    before = group_down * ROWS + down < group_across * ROWS + across
    rank = jnp.sum(before.astype(jnp.int32), axis=0, keepdims=True)
    sort = (rank == down).astype(BF16)
    sort_ref[...] = sort
    order = ((down % 8) * CHIPS + down // 8 == across).astype(BF16)
    unsort_ref[...] = lax.dot_general(order, sort, NT, preferred_element_type=F32).astype(BF16)
    mark = lax.broadcasted_iota(jnp.int32, (ROWS, 128), 1)
    place = lax.broadcasted_iota(jnp.int32, (ROWS, 128), 0) - chip_ref[0] * 8
    own = (place >= 0) & (place < 8)
    marks = (mark == 16 + group_down) | (own & (mark == 32 + place)) | (jnp.logical_not(own) & (mark == 40))
    marks_ref[...] = jnp.dot(sort, marks.astype(BF16), preferred_element_type=F32)
    for copy in outgoing[3:6]:
        copy.start()
    longest = jnp.zeros((PAGE, 1), F32)
    for n, group_at in ((0, None), (2, 0), (1, None), (3, 4)):
        source = (0, 4, 2, 6)[n]
        incoming[source].wait()
        incoming[source + 1].wait()
        for j in range(4):
            rows = slice((4 * n + j) * PAGE, (4 * n + j + 1) * PAGE)
            key = held[source][j * PAGE : (j + 1) * PAGE, :]
            wide = key.astype(F32)
            longest = jnp.maximum(longest, jnp.sum(wide * wide, axis=1, keepdims=True))
            more = (lane < 8).astype(F32)
            if group_at is not None:
                hidden = (lane >= 16) & (lane < 32) & (lane != 16 + groups_ref[group_at + j])
                more = jnp.where(hidden, NEG, more)
            keys_ref[rows, :HD] = key
            keys_ref[rows, HD:] = more.astype(BF16)
            values_ref[rows, :HD] = held[source + 1][j * PAGE : (j + 1) * PAGE, :]
            values_ref[rows, HD:] = ones
        outgoing[6 + 2 * n].start()
        outgoing[7 + 2 * n].start()
    incoming[8].wait()
    incoming[9].wait()
    new_lane = lax.broadcasted_iota(jnp.int32, (16, 128), 1)
    new_token = lax.broadcasted_iota(jnp.int32, (16, 128), 0)
    blank = jnp.zeros((12, HD), F32)
    longest_own = longest
    for j in range(2):
        here = (lane >= 32 + 4 * j) & (lane < 36 + 4 * j)
        other_row = (lane >= 32) & (lane <= 40) & jnp.logical_not(here)
        for n in range(SUFFIX // PAGE):
            rows = slice(n * PAGE, (n + 1) * PAGE)
            token = lax.broadcasted_iota(jnp.int32, (PAGE, 128), 0) + n * PAGE
            hidden = other_row | (here & (token >= lengths_ref[j]))
            key = suffix_keys_ref[j, rows, :]
            wide = key.astype(F32)
            longest_own = jnp.maximum(longest_own, jnp.sum(wide * wide, axis=1, keepdims=True))
            own_keys_ref[j, rows, :HD] = key
            own_keys_ref[j, rows, HD:] = jnp.where(hidden, NEG, (lane < 8).astype(F32)).astype(BF16)
            own_values_ref[j, rows, :HD] = suffix_values_ref[j, rows, :]
            own_values_ref[j, rows, HD:] = ones
        seen = (new_lane >= 32 + 4 * j) & (new_lane < 36 + 4 * j) & (new_token <= new_lane - (32 + 4 * j))
        hidden = (new_lane >= 32) & (new_lane <= 40) & jnp.logical_not(seen)
        wide = new_keys_ref[j].astype(F32)
        longest_own = jnp.maximum(longest_own, jnp.max(jnp.sum(wide * wide, axis=1, keepdims=True)))
        own_keys_ref[j, SUFFIX:, :HD] = jnp.concatenate([wide, blank], axis=0).astype(BF16)
        own_keys_ref[j, SUFFIX:, HD:] = jnp.where(hidden, NEG, (new_lane < 8).astype(F32)).astype(BF16)
        own_values_ref[j, SUFFIX:, :HD] = jnp.concatenate([new_values_ref[j].astype(F32), blank], axis=0).astype(BF16)
        own_values_ref[j, SUFFIX:, HD:] = ones[:16]
    longest_ref[0:1, :] = jnp.broadcast_to(jnp.sqrt(jnp.max(longest)) * 1.02, (1, 128))
    longest_ref[1:2, :] = jnp.broadcast_to(jnp.sqrt(jnp.max(longest_own)) * 1.02, (1, 128))
    longest_ref[2:8, :] = jnp.zeros((6, 128), F32)
    for copy in outgoing[:3]:
        copy.start()
    for copy in outgoing:
        copy.wait()


def attend_kernel(
    at_ref, *refs,
):
    sources, out_ref, (q_rows, shift_ref, total_ref, sent_ref), held, sems = (
        refs[:9], refs[9], refs[10:14], refs[14:23], refs[23]
    )
    keys_ref, values_ref, own_keys_ref, own_values_ref, longest_ref, sort_ref, unsort_ref, marks_ref, q_ref = held
    copies = copies_of(list(zip(sources, held)), sems)
    for i in (8, 5, 7, 4, 0, 1, 2, 3, 6):
        copies[i].start()
    for i in (8, 5, 7, 4):
        copies[i].wait()
    lane = lax.broadcasted_iota(jnp.int32, (ROWS, 128), 1)
    q_all = jnp.dot(sort_ref[...], q_ref[...], preferred_element_type=F32)
    by_head = lax.broadcasted_iota(jnp.int32, (WIDTH, 128), 0) // HD == lax.broadcasted_iota(jnp.int32, (WIDTH, 128), 1)
    squares = jnp.dot((q_all * q_all).astype(BF16), by_head.astype(BF16), preferred_element_type=F32)
    marks = marks_ref[...]
    longest = jnp.where(marks[:, 40:41] > 0.5, longest_ref[0:1, :], longest_ref[1:2, :])
    shift = (jnp.sqrt(squares) * longest).astype(BF16).astype(F32)
    shift_ref[...] = shift
    for h in range(HEADS):
        q_rows[h, :, :HD] = q_all[:, h * HD : (h + 1) * HD].astype(BF16)
        q_rows[h, :, HD:] = jnp.where(lane == h, -shift, marks).astype(BF16)

    def powers(q, keys, more=0.0):
        return jnp.exp2(lax.dot_general(q, keys, NT, preferred_element_type=F32) * SCALE + more).astype(BF16)

    def taken(j, row, size, keys, values, more=0.0):
        rows = pl.ds(pl.multiple_of(row, 16), size)
        q = q_rows[:, rows, :].reshape(HEADS * size, 2 * HD)
        return rows, size, jnp.dot(powers(q, keys, more), values, preferred_element_type=F32)

    def add(rows, size, added):
        total_ref[:, rows, :] += added.reshape(HEADS, size, 2 * HD)

    def page(j):
        return pl.ds(pl.multiple_of(PROMPT + j * PAGE, PAGE), PAGE)

    for i in (0, 1, 2, 3, 6):
        copies[i].wait()
    for h in range(HEADS):
        power = powers(q_rows[h], keys_ref[:PROMPT, :])
        total_ref[h] = jnp.dot(power, values_ref[:PROMPT, :], preferred_element_type=F32)
    firsts = [jnp.minimum(lax.div(at_ref[j], 16) * 16, ROWS - WINDOW) for j in range(8)]
    parts = [taken(j, firsts[j], WINDOW, keys_ref[page(j), :], values_ref[page(j), :]) for j in range(8)]
    parts += [
        taken(j, lax.div(at_ref[16 + j], 16) * 16, 16, own_keys_ref[j], own_values_ref[j]) for j in range(2)
    ]
    for part in parts:
        add(*part)

    def rest(j, _):
        first = jnp.minimum(lax.div(at_ref[j], 16) * 16, ROWS - WINDOW) + WINDOW
        left = at_ref[8 + j] - first

        def more_rows(i, _):
            wanted = first + i * WINDOW
            row = jnp.minimum(wanted, ROWS - WINDOW)
            done = lax.broadcasted_iota(jnp.int32, (HEADS, WINDOW, 1), 1) + row < wanted
            hide = jnp.where(done, NEG, 0.0).reshape(HEADS * WINDOW, 1)
            add(*taken(j, row, WINDOW, keys_ref[page(j), :], values_ref[page(j), :], hide))
            return 0

        lax.fori_loop(0, jnp.where(left > 0, lax.div(left + WINDOW - 1, WINDOW), 0), more_rows, 0)
        return 0

    lax.fori_loop(0, 8, rest, 0)

    def masses():
        mass = jnp.ones((ROWS, 128), F32)
        for h in range(HEADS):
            mass = jnp.where(lane == h, total_ref[h, :, HD:], mass)
        return mass

    @pl.when(jnp.min(masses()) < 2.0**-90)
    def _():
        def one_head(h, _):
            def scores(keys):
                return lax.dot_general(q_rows[h], keys, NT, preferred_element_type=F32)

            def some(c):
                return pl.ds(pl.multiple_of(c * 1024, 1024), 1024)

            def peak_of(c, peak):
                return jnp.maximum(peak, jnp.max(scores(keys_ref[some(c), :]), axis=1, keepdims=True))

            peak = lax.fori_loop(0, KEYS // 1024, peak_of, jnp.full((ROWS, 1), -3e38, F32))
            for j in range(2):
                peak = jnp.maximum(peak, jnp.max(scores(own_keys_ref[j]), axis=1, keepdims=True))
            total_ref[h] = jnp.zeros((ROWS, 2 * HD), F32)

            def add_some(keys, values):
                power = jnp.exp2((scores(keys) - peak) * SCALE).astype(BF16)
                total_ref[h] += jnp.dot(power, values, preferred_element_type=F32)

            def add_chunk(c, _):
                add_some(keys_ref[some(c), :], values_ref[some(c), :])
                return 0

            lax.fori_loop(0, KEYS // 1024, add_chunk, 0)
            for j in range(2):
                add_some(own_keys_ref[j], own_values_ref[j])
            shift_ref[...] += jnp.where(lane == h, peak, 0.0)
            return 0

        lax.fori_loop(0, HEADS, one_head, 0)

    for h in range(HEADS):
        sent_ref[:, h * HD : (h + 1) * HD] = (total_ref[h, :, :HD] / total_ref[h, :, HD:]).astype(BF16)
    lse = jnp.where(lane < HEADS, shift_ref[...] * SCALE + jnp.log2(masses()), 0.0)
    high, middle, low = split3(lse)
    sent_ref[:, WIDTH:] = (high + pltpu.roll(middle, 8, 1) + pltpu.roll(low, 16, 1)).astype(BF16)
    out_ref[...] = jnp.dot(unsort_ref[...], sent_ref[...], preferred_element_type=F32).astype(BF16)


def merge_kernel(came_ref, out_ref, rows_ref):
    parts = came_ref[:, :, WIDTH:].astype(F32)
    lse = parts + pltpu.roll(parts, 120, 2) + pltpu.roll(parts, 112, 2)
    top = jnp.max(lse, axis=0, keepdims=True)
    weights = jnp.exp2(lse - top)
    weights = weights / jnp.sum(weights, axis=0, keepdims=True)
    for h in range(HEADS):
        rows = came_ref[:, :, h * HD : (h + 1) * HD].astype(F32)
        rows_ref[:, h, :] = jnp.sum(rows * weights[:, :, h : h + 1], axis=0)
    rows = rows_ref[...].astype(BF16)
    for z in range(Z):
        out_ref[z] = rows


def project(rank_ref, rows_ref, weight_refs):
    total = 0.0
    for j, offset in enumerate(OFFSETS):
        block = lax.rem(rank_ref[0] + offset, T)
        rows = rows_ref[:, pl.ds(pl.multiple_of(block * WIDTH, WIDTH), WIDTH)]
        ref, at = WEIGHT_AT[j]
        total = total + lax.dot_general(rows, weight_refs[ref][at], NT, preferred_element_type=F32)
    return total


def project_mine_kernel(rank_ref, rows_ref, w0, w1, w2, w3, w4, out_ref):
    out_ref[...] = project(rank_ref, rows_ref, (w0, w1, w2, w3, w4))


def project_all_kernel(rank_ref, core_ref, rows_ref, w0, w1, w2, w3, w4, mine_ref, out_ref):
    theirs, mine = project(rank_ref, rows_ref, (w0, w1, w2, w3, w4)), mine_ref[...]
    even = jnp.where(core_ref[0] == 0, mine, theirs)
    odd = jnp.where(core_ref[0] == 0, theirs, mine)
    pieces = []
    for x in range(X):
        pieces += [even[x * Z : (x + 1) * Z], odd[x * Z : (x + 1) * Z]]
    out_ref[...] = jnp.concatenate(pieces, axis=0).astype(BF16)


def spread(queries):
    return pl.pallas_call(
        spread_kernel,
        out_shape=jax.ShapeDtypeStruct((CHIPS, 8, WIDTH), BF16),
        in_specs=[VMEM],
        out_specs=VMEM,
        compiler_params=PARAMS,
    )(queries)


PREPARED = [
    ((KEYS, 2 * HD), BF16),
    ((KEYS, 2 * HD), BF16),
    ((2, SUFFIX + 16, 2 * HD), BF16),
    ((2, SUFFIX + 16, 2 * HD), BF16),
    ((8, 128), F32),
    ((ROWS, ROWS), BF16),
    ((ROWS, ROWS), BF16),
    ((ROWS, 128), F32),
]


def prepare(*args):
    return pl.pallas_call(
        prep_kernel,
        out_shape=[jax.ShapeDtypeStruct(*each) for each in PREPARED],
        in_specs=[SMEM] * 3 + [VMEM] * 3 + [HBM] * 7,
        out_specs=[HBM] * 8,
        scratch_shapes=[pltpu.VMEM((1024, HD), BF16)] * 8
        + [pltpu.VMEM((2, SUFFIX, HD), BF16)] * 2
        + [pltpu.VMEM(*each) for each in PREPARED]
        + [pltpu.SemaphoreType.DMA((10,)), pltpu.SemaphoreType.DMA((14,))],
        compiler_params=PARAMS,
        cost_estimate=pl.CostEstimate(flops=1, bytes_accessed=1, transcendentals=0),
    )(*args)


def attend(*args):
    return pl.pallas_call(
        attend_kernel,
        out_shape=jax.ShapeDtypeStruct((ROWS, PACKED), BF16),
        in_specs=[SMEM] + [HBM] * 9,
        out_specs=VMEM,
        scratch_shapes=[
            pltpu.VMEM((HEADS, ROWS, 2 * HD), BF16),
            pltpu.VMEM((ROWS, 128), F32),
            pltpu.VMEM((HEADS, ROWS, 2 * HD), F32),
            pltpu.VMEM((ROWS, PACKED), BF16),
        ]
        + [pltpu.VMEM(*each) for each in PREPARED]
        + [pltpu.VMEM((ROWS, WIDTH), BF16), pltpu.SemaphoreType.DMA((9,))],
        compiler_params=pltpu.CompilerParams(vmem_limit_bytes=62_800_000),
    )(*args)


def local(
    queries,
    prompt_keys,
    prompt_values,
    pool_keys,
    pool_values,
    suffix_keys,
    suffix_values,
    new_keys,
    new_values,
    suffix_lengths,
    branch_group,
    page_list,
    out_weight,
):
    page, rank = lax.axis_index("page"), lax.axis_index("tensor").reshape(1)
    core, chip = lax.rem(page, 2), lax.div(page, 2)
    sent, prompt_keys, pool_keys, prompt_values, pool_values = lax.optimization_barrier(
        (spread(queries), prompt_keys, pool_keys, prompt_values, pool_values)
    )
    gathered = lax.all_to_all(sent, "page", 0, 0, tiled=True, axis_index_groups=XZ_GROUPS)
    gathered = gathered.reshape(ROWS, WIDTH)
    row_group = lax.dynamic_index_in_dim(branch_group.reshape(CHIPS, 2, 2), core, 1, keepdims=False)
    row_group = jnp.repeat(row_group.reshape(-1), 4)
    order = row_group * ROWS + jnp.arange(ROWS)
    page_ids = jnp.concatenate([page * 4 + jnp.arange(4), (page ^ 1) * 4 + jnp.arange(4)])
    matched = page_list[:, :, None] == page_ids[None, None, :]
    page_group = jnp.sum(
        jnp.where(matched, jnp.arange(page_list.shape[0])[:, None, None], 0), axis=(0, 1)
    )
    own_group = lax.dynamic_slice_in_dim(branch_group, 2 * page, 2)
    limits = jnp.concatenate(
        [page_group * ROWS, (page_group + 1) * ROWS, own_group * ROWS + chip * 8 + jnp.arange(2) * 4]
    )
    at = jnp.sum((order[:, None] < limits[None, :]).astype(jnp.int32), axis=0)
    own_pages = [prompt_keys, prompt_values, pool_keys, pool_values]
    other_pages = lax.ppermute(jnp.concatenate(own_pages, axis=0), "page", CORE_SWAP)
    def from_rank(offset, array):
        return lax.ppermute(array, "tensor", [(t, (t - offset) % T) for t in range(T)])

    weight, other_pages = lax.optimization_barrier((out_weight.T[None], other_pages))
    across, after, before = from_rank(4, weight), from_rank(2, weight), from_rank(6, weight)
    prepared = prepare(
        chip.reshape(1), page_group, suffix_lengths, row_group.reshape(1, ROWS), new_keys, new_values,
        *own_pages, other_pages, suffix_keys, suffix_values,
    )
    gathered, across = lax.optimization_barrier((gathered, across))
    packed = attend(at, *prepared, gathered)
    packed, weight = lax.optimization_barrier((packed, weight))
    two = jnp.concatenate([weight, across], axis=0)
    next_two, last_two = from_rank(1, two), from_rank(7, two)
    came_rows = lax.all_to_all(
        packed.reshape(CHIPS, 8, PACKED), "page", 0, 0, tiled=True, axis_index_groups=XZ_GROUPS
    )
    weights = [two, after, before, next_two, last_two]
    came_rows, *weights = lax.optimization_barrier((came_rows, *weights))
    rows = pl.pallas_call(
        merge_kernel,
        out_shape=jax.ShapeDtypeStruct((Z, T, HEADS, HD), BF16),
        in_specs=[VMEM],
        out_specs=VMEM,
        scratch_shapes=[pltpu.VMEM((8, HEADS, HD), F32)],
        compiler_params=SMALL,
    )(came_rows)
    rows = lax.all_to_all(
        rows.reshape(Z * T, HEADS, HD), ("page", "tensor"), 0, 0, tiled=True, axis_index_groups=ZT_GROUPS
    )
    rows = jnp.broadcast_to(rows.reshape(1, Z, T * WIDTH), (X, Z, T * WIDTH))
    rows = lax.all_to_all(rows, "page", 0, 0, tiled=True, axis_index_groups=X_GROUPS)
    rows = rows.reshape(CHIPS, T * WIDTH)
    rows_other = lax.ppermute(rows, "page", CORE_SWAP)
    columns = out_weight.shape[1]
    mine = pl.pallas_call(
        project_mine_kernel,
        out_shape=jax.ShapeDtypeStruct((CHIPS, columns), F32),
        in_specs=[SMEM] + [VMEM] * 6,
        out_specs=VMEM,
        compiler_params=SMALL,
    )(rank, rows, *weights)
    return pl.pallas_call(
        project_all_kernel,
        out_shape=jax.ShapeDtypeStruct((2 * CHIPS, columns), BF16),
        in_specs=[SMEM] * 2 + [VMEM] * 7,
        out_specs=VMEM,
        compiler_params=SMALL,
    )(rank, core.reshape(1), rows_other, *weights, mine)


def solution(mesh):
    placed = (
        P("page", None, "tensor"),
        P("page", "tensor"),
        P("page", "tensor"),
        P("page", "tensor"),
        P("page", "tensor"),
        P("page", None, "tensor"),
        P("page", None, "tensor"),
        P("page", None, "tensor"),
        P("page", None, "tensor"),
        P("page"),
        P(),
        P(),
        P("tensor", "page"),
    )
    return jax.shard_map(
        local, mesh=mesh, in_specs=placed, out_specs=P("tensor", "page"), check_vma=False
    )
```

time: 131 us -> 162 us (1.24)
  Pallas kernels: 17.5 us -> 61.8 us
  starting transfers between devices: 22.8 us -> 52.6 us
  blocking collectives: 56.1 us -> 33.4 us
  between operations: 13.7 us -> 0.25 us
  waiting for transfers between devices: 13.1 us -> 8.55 us
  matrix products: 2.9 us -> 0 us
    pallas_call x1 -> x5, Pallas kernels: 15.2 us -> 61.3 us  [the longest x1 53.4 us: attend(): pl.pallas_call(attend_kernel, out_shape=jax.ShapeDtypeStruct((ROWS, PACKE...]
    all_to_all x1 -> x0, blocking collectives: 23 us -> none  [local(): lax.all_to_all(packed.reshape(CHIPS, 8, PACKED), 'page', 0, 0, tiled=True...]
    ppermute x1 -> x6, starting transfers between devices: 8.92 us -> 30.1 us  [the longest x5 21.3 us: from_rank(): lax.ppermute(array, 'tensor', [(t, (t - offset) % T) for t in range(T)])]
    all_to_all x1, waiting for transfers between devices: 12.4 us -> 0.1 us  [local(): lax.all_to_all(sent, 'page', 0, 0, tiled=True, axis_index_groups=XZ_GROUPS)]
    all_to_all x0 -> x1, starting transfers between devices: none -> 8.47 us  [local(): lax.all_to_all(packed.reshape(CHIPS, 8, PACKED), 'page', 0, 0, tiled=True...]
    ppermute x1 -> x6, waiting for transfers between devices: 0.01 us -> 7.4 us  [the longest x5 7.4 us: from_rank(): lax.ppermute(array, 'tensor', [(t, (t - offset) % T) for t in range(T)])]
    dot_general x4 -> x0, matrix products: 2.9 us -> none  [the longest x1 1.89 us: local(): jnp.dot(rows, weight, preferred_element_type=F32).astype(BF16)]
    pallas_call x1, Pallas kernels: 2.25 us -> 0.52 us  [local(): pl.pallas_call(merge_kernel, out_shape=jax.ShapeDtypeStruct((Z, T, HEADS,...]
  transfers between devices with their start and end apart: 4 -> 9, of which waited for: 1 -> 4; matrix products, arithmetic and copies ran while one was open for 3% -> 2% of each run, Pallas kernels for 13% -> 3%
where the time goes in v2:
time: 162 us; the launch traced here: 161 us
  Pallas kernels  61.8 us (38%)
  starting transfers between devices  52.6 us (32%)
  blocking collectives  33.4 us (21%)
  waiting for transfers between devices  8.55 us (5%)
  other arithmetic  2.46 us (2%)
  local copies, waits for them, and re-layouts  2.18 us (1%)
    pallas_call x1, Pallas kernels, attend(): pl.pallas_call(attend_kernel, out_shape=jax.ShapeDtypeStruct((ROWS, PACKE...  53.4 us
    all_to_all x1, blocking collectives, local(): lax.all_to_all(rows.reshape(Z * T, HEADS, HD), ('page', 'tensor'), 0, 0,...  22.7 us
    ppermute x5, starting transfers between devices, from_rank(): lax.ppermute(array, 'tensor', [(t, (t - offset) % T) for t in range(T)])  21.3 us
    all_to_all x1, blocking collectives, local(): lax.all_to_all(rows, 'page', 0, 0, tiled=True, axis_index_groups=X_GROUPS)  10.7 us
    ppermute x1, starting transfers between devices, local(): lax.ppermute(jnp.concatenate(own_pages, axis=0), 'page', CORE_SWAP)  8.78 us
    all_to_all x1, starting transfers between devices, local(): lax.all_to_all(packed.reshape(CHIPS, 8, PACKED), 'page', 0, 0, tiled=True...  8.47 us
    all_to_all x1, starting transfers between devices, local(): lax.all_to_all(sent, 'page', 0, 0, tiled=True, axis_index_groups=XZ_GROUPS)  7.53 us
    ppermute x5, waiting for transfers between devices, from_rank(): lax.ppermute(array, 'tensor', [(t, (t - offset) % T) for t in range(T)])  7.4 us
  transfers between devices with their start and end apart: 9, of which 4 were waited for; matrix products, arithmetic and copies ran while one was open for 2% of the time, Pallas kernels for 3%

profile of v2, /device:TPU:1, one launch (start us, length us, event | category | flops | bytes accessed | tf_op | source)
XLA Modules:
  0.0 161.3 jit_solution(12250365080735882197)
XLA Ops:
  0.0 0.0 copy-start.5
  0.0 1.6 %shard_map.127 = bf16[32,8,1024]{2,1,0:T(8,128)(2,1)} custom-call(bf16[2,4,1024]{2,1,0:T(4,128)(2,1)} %q_ref.1), custom_call_target="tpu_custom_call" | custom-call | tf_op jit(solution)/shard_map/pallas_call | solution.py:312
  1.6 1.3 pad_maximum_fusion
  2.9 8.8 %collective-permute-start = (bf16[4096,128]{1,0:T(8,128)(2,1)S(1)}, bf16[4096,128]{1,0:T(8,128)(2,1)S(1)}, u32[]{:S(2)}, u32[]{:S(2)}) collective-permute-start(bf16[4096,128]{1,0:T(8,128)(2,1)S(1)} %pad_maximum_fusion), channel_id=1, source_target_pairs={{0,8},{8,0},{16,24},{24,16},{32,40},{40,32},{48,56},{56,48},{64,72... | collective-permute-start | bytes 3145736 | tf_op jit(solution)/shard_map/ppermute | solution.py:402
  11.7 7.5 %all-to-all-start = ((bf16[32,8,1024]{2,1,0:T(8,128)(2,1)}), bf16[32,8,1024]{2,1,0:T(8,128)(2,1)S(1)}, u32[]{:S(2)}, u32[]{:S(2)}) async-start(bf16[32,8,1024]{2,1,0:T(8,128)(2,1)} %shard_map.127), calls=%async_computation | async-start | bytes 1048576 | tf_op jit(solution)/shard_map/all_to_all | solution.py:386
  19.2 0.0 copy-done.5
  19.2 0.2 reshape.47
  19.4 0.1 dynamic-slice_reduce_fusion
  19.5 0.1 reshape.48
  19.6 0.1 multiply_add_fusion
  19.7 0.1 broadcast_in_dim.32
  19.7 0.1 mul.40
  19.9 0.1 pad_add_fusion
  19.9 0.0 copy-done.3
  19.9 0.2 select_reduce_fusion.groups_ref
  20.2 0.0 collective-permute-done.refs_4_
  20.2 0.0 copy-start.1
  20.2 0.0 copy-done.2
  20.2 7.5 %collective-permute-start.1 = (bf16[1,80,1024]{2,1,0:T(8,128)(2,1)S(1)}, bf16[1,80,1024]{2,1,0:T(8,128)(2,1)S(1)}, u32[]{:S(2)}, u32[]{:S(2)}) collective-permute-start(bf16[1,80,1024]{2,1,0:T(8,128)(2,1)S(1)} %bitcast.15), channel_id=1, source_target_pairs={{0,4},{1,5},{2,6},{3,7},{4,0},{5,1},{6,2},{7,3},{8,12},{9,13},{10,... | collective-permute-start | bytes 491528 | tf_op jit(solution)/shard_map/ppermute | solution.py:404
  27.7 0.1 pad_add_fusion.1
  27.7 0.1 broadcast_in_dim.35
  27.8 0.7 reshape_reshape.3.row_group_ref
  28.5 0.8 convert_reduce_fusion.at_ref
  29.3 0.0 copy-done.4
  29.3 0.0 copy-done.1
  29.3 4.7 %shard_map.128 = (bf16[4096,256]{1,0:T(8,128)(2,1)}, bf16[4096,256]{1,0:T(8,128)(2,1)}, bf16[2,528,256]{2,1,0:T(8,128)(2,1)}, bf16[2,528,256]{2,1,0:T(8,128)(2,1...) custom-call(s32[1]{0:T(128)} %bitcast.2.chip_ref, ...), custom_call_target="tpu_custom_call" | custom-call | flops 1 | bytes 1 | tf_op jit(solution)/shard_map/pallas_call | solution.py:334
  34.0 0.1 all-to-all-done
  34.1 0.0 collective-permute-done.1
  34.1 0.8 copy-done
  34.9 53.4 %shard_map.129 = bf16[256,1152]{1,0:T(8,128)(2,1)} custom-call(s32[18]{0:T(128)} %convert_reduce_fusion.at_ref, bf16[4096,256]{1,0:T(8,128)(2,1)} %get-tuple-element.35.refs_0_, bf16[4096,256]{1,0:T(8,128)(2,1)} %get-tuple-element.36.refs_1_, bf16[2,528,256]{2,1,0:T(8,128)(2,1)} %get-tuple-element.37.refs_2_, ...), custom_call_target="tpu_custom_call" | custom-call | tf_op jit(solution)/shard_map/pallas_call | solution.py:349
  88.3 8.5 %all-to-all-start.1 = ((bf16[32,8,1152]{2,1,0:T(8,128)(2,1)}), bf16[32,8,1152]{2,1,0:T(8,128)(2,1)S(1)}, u32[]{:S(2)}, u32[]{:S(2)}) async-start(bf16[32,8,1152]{2,1,0:T(8,128)(2,1)} %bitcast.13), calls=%async_computation.1 | async-start | bytes 1179648 | tf_op jit(solution)/shard_map/all_to_all | solution.py:417
  96.8 5.7 %collective-permute-start.4 = (bf16[2,80,1024]{2,1,0:T(8,128)(2,1)S(1)}, bf16[2,80,1024]{2,1,0:T(8,128)(2,1)S(1)}, u32[]{:S(2)}, u32[]{:S(2)}) collective-permute-start(bf16[2,80,1024]{2,1,0:T(8,128)(2,1)S(1)} %constant_dynamic-update-slice_fusion.w0), channel_id=1, source_target_pairs={{0,7},{1,0},{2,1},{3,2},{4,3},{5,4},{6,5},{7,6},{8,15},{9,8},{10,9... | collective-permute-start | bytes 983048 | tf_op jit(solution)/shard_map/ppermute | solution.py:404
  102.6 1.9 %collective-permute-start.5 = (bf16[2,80,1024]{2,1,0:T(8,128)(2,1)S(1)}, bf16[2,80,1024]{2,1,0:T(8,128)(2,1)S(1)}, u32[]{:S(2)}, u32[]{:S(2)}) collective-permute-start(bf16[2,80,1024]{2,1,0:T(8,128)(2,1)S(1)} %constant_dynamic-update-slice_fusion.w0), channel_id=1, source_target_pairs={{0,1},{1,2},{2,3},{3,4},{4,5},{5,6},{6,7},{7,0},{8,9},{9,10},{10,1... | collective-permute-start | bytes 983048 | tf_op jit(solution)/shard_map/ppermute | solution.py:404
  104.5 3.3 %collective-permute-start.2 = (bf16[1,80,1024]{2,1,0:T(8,128)(2,1)S(1)}, bf16[1,80,1024]{2,1,0:T(8,128)(2,1)S(1)}, u32[]{:S(2)}, u32[]{:S(2)}) collective-permute-start(bf16[1,80,1024]{2,1,0:T(8,128)(2,1)S(1)} %bitcast.17), channel_id=1, source_target_pairs={{0,6},{1,7},{2,0},{3,1},{4,2},{5,3},{6,4},{7,5},{8,14},{9,15},{10,... | collective-permute-start | bytes 491528 | tf_op jit(solution)/shard_map/ppermute | solution.py:404
  107.8 2.9 %collective-permute-start.3 = (bf16[1,80,1024]{2,1,0:T(8,128)(2,1)S(1)}, bf16[1,80,1024]{2,1,0:T(8,128)(2,1)S(1)}, u32[]{:S(2)}, u32[]{:S(2)}) collective-permute-start(bf16[1,80,1024]{2,1,0:T(8,128)(2,1)S(1)} %bitcast.18), channel_id=1, source_target_pairs={{0,2},{1,3},{2,4},{3,5},{4,6},{5,7},{6,0},{7,1},{8,10},{9,11},{10,... | collective-permute-start | bytes 491528 | tf_op jit(solution)/shard_map/ppermute | solution.py:404
  110.7 3.4 %collective-permute-done.2.w1 = bf16[1,80,1024]{2,1,0:T(8,128)(2,1)S(1)} collective-permute-done((bf16[1,80,1024]{2,1,0:T(8,128)(2,1)S(1)}, bf16[1,80,1024]{2,1,0:T(8,128)(2,1)S(1)}, u32[]{:S(2)}, u32[]{:S(2)}) %collective-permute-start.2) | collective-permute-done | bytes 163872 | tf_op jit(solution)/shard_map/ppermute | solution.py:404
  114.1 4.0 %collective-permute-done.3.w2 = bf16[1,80,1024]{2,1,0:T(8,128)(2,1)S(1)} collective-permute-done((bf16[1,80,1024]{2,1,0:T(8,128)(2,1)S(1)}, bf16[1,80,1024]{2,1,0:T(8,128)(2,1)S(1)}, u32[]{:S(2)}, u32[]{:S(2)}) %collective-permute-start.3) | collective-permute-done | bytes 163872 | tf_op jit(solution)/shard_map/ppermute | solution.py:404
  118.1 0.0 collective-permute-done.4.w3
  118.1 0.0 collective-permute-done.5.w4
  118.1 0.0 all-to-all-done.1.came_ref
  118.1 0.5 shard_map.130
  118.6 22.7 %all_to_all.20 = bf16[64,8,128]{2,1,0:T(8,128)(2,1)S(1)} all-to-all(bf16[64,8,128]{2,1,0:T(8,128)(2,1)S(1)} %bitcast.12), channel_id=1, replica_groups={{0,1,2,3,4,5,6,7,16,17,18,19,20,21,22,23,32,33,34,35,36,37,38,39,48,49,..., dimensions={0} | all-to-all | bytes 262144 | tf_op jit(solution)/shard_map/all_to_all | solution.py:430
  141.3 0.1 broadcast_in_dim.37
  141.4 10.7 %all_to_all.21 = bf16[4,8,8192]{2,1,0:T(8,128)(2,1)S(1)} all-to-all(bf16[4,8,8192]{2,1,0:T(8,128)(2,1)S(1)} %broadcast_in_dim.38), channel_id=1, replica_groups={{0,128,256,384},{8,136,264,392},{16,144,272,400},{24,152,280,408},{32,1..., dimensions={0} | all-to-all | bytes 1048576 | tf_op jit(solution)/shard_map/all_to_all | solution.py:434
  152.1 6.5 %collective-permute-start.6 = (bf16[32,8192]{1,0:T(8,128)(2,1)S(1)}, bf16[32,8192]{1,0:T(8,128)(2,1)S(1)}, u32[]{:S(2)}, u32[]{:S(2)}) collective-permute-start(bf16[32,8192]{1,0:T(8,128)(2,1)S(1)} %bitcast.10), channel_id=1, source_target_pairs={{0,8},{8,0},{16,24},{24,16},{32,40},{40,32},{48,56},{56,48},{64,72... | collective-permute-start | bytes 1572872 | tf_op jit(solution)/shard_map/ppermute | solution.py:436
  158.7 0.5 shard_map.131.mine_ref
  159.1 1.0 collective-permute-done.6.rows_ref
  160.2 1.1 shard_map.132
  (11 shorter events, 0.1 us)
Async XLA Ops:
  0.0 19.2 %copy-start.5 = (s32[128]{0:T(128)S(1)}, s32[128]{0:T(128)}, u32[]{:S(2)}) copy-start(s32[128]{0:T(128)} %param.23) | copy-start | bytes 1540
  0.0 19.9 %copy-start.3 = (s32[16,16]{1,0:T(8,128)S(1)}, s32[16,16]{1,0:T(8,128)}, u32[]{:S(2)}) copy-start(s32[16,16]{1,0:T(8,128)} %param.24) | copy-start | bytes 3076
  0.0 20.2 %copy-start.2 = (bf16[1024,80]{0,1:T(8,128)(2,1)S(1)}, bf16[1024,80]{0,1:T(8,128)(2,1)}, u32[]{:S(2)}) copy-start(bf16[1024,80]{0,1:T(8,128)(2,1)} %param.25) | copy-start | bytes 491524
  2.9 17.3 %collective-permute-start = (bf16[4096,128]{1,0:T(8,128)(2,1)S(1)}, bf16[4096,128]{1,0:T(8,128)(2,1)S(1)}, u32[]{:S(2)}, u32[]{:S(2)}) collective-permute-start(bf16[4096,128]{1,0:T(8,128)(2,1)S(1)} %pad_maximum_fusion), channel_id=1, source_target_pairs={{0,8},{8,0},{16,24},{24,16},{32,40},{40,32},{48,56},{56,48},{64,72... | collective-permute-start | bytes 3145736 | tf_op jit(solution)/shard_map/ppermute | solution.py:402
  11.7 22.4 %all-to-all-start = ((bf16[32,8,1024]{2,1,0:T(8,128)(2,1)}), bf16[32,8,1024]{2,1,0:T(8,128)(2,1)S(1)}, u32[]{:S(2)}, u32[]{:S(2)}) async-start(bf16[32,8,1024]{2,1,0:T(8,128)(2,1)} %shard_map.127), calls=%async_computation | async-start | bytes 1048576 | tf_op jit(solution)/shard_map/all_to_all | solution.py:386
  20.1 9.1 %copy-start.4 = (s32[8]{0:T(128)}, s32[8]{0:T(128)S(1)}, u32[]{:S(2)}) copy-start(s32[8]{0:T(128)S(1)} %select_reduce_fusion.groups_ref) | copy-start | bytes 100
  20.2 9.1 %copy-start.1 = (bf16[4096,128]{1,0:T(8,128)(2,1)}, bf16[4096,128]{1,0:T(8,128)(2,1)S(1)}, u32[]{:S(2)}) copy-start(bf16[4096,128]{1,0:T(8,128)(2,1)S(1)} %collective-permute-done.refs_4_) | copy-start | bytes 3145732
  20.2 13.9 %collective-permute-start.1 = (bf16[1,80,1024]{2,1,0:T(8,128)(2,1)S(1)}, bf16[1,80,1024]{2,1,0:T(8,128)(2,1)S(1)}, u32[]{:S(2)}, u32[]{:S(2)}) collective-permute-start(bf16[1,80,1024]{2,1,0:T(8,128)(2,1)S(1)} %bitcast.15), channel_id=1, source_target_pairs={{0,4},{1,5},{2,6},{3,7},{4,0},{5,1},{6,2},{7,3},{8,12},{9,13},{10,... | collective-permute-start | bytes 491528 | tf_op jit(solution)/shard_map/ppermute | solution.py:404
  34.1 0.8 copy-start
  88.3 29.8 %all-to-all-start.1 = ((bf16[32,8,1152]{2,1,0:T(8,128)(2,1)}), bf16[32,8,1152]{2,1,0:T(8,128)(2,1)S(1)}, u32[]{:S(2)}, u32[]{:S(2)}) async-start(bf16[32,8,1152]{2,1,0:T(8,128)(2,1)} %bitcast.13), calls=%async_computation.1 | async-start | bytes 1179648 | tf_op jit(solution)/shard_map/all_to_all | solution.py:417
  96.8 21.3 %collective-permute-start.4 = (bf16[2,80,1024]{2,1,0:T(8,128)(2,1)S(1)}, bf16[2,80,1024]{2,1,0:T(8,128)(2,1)S(1)}, u32[]{:S(2)}, u32[]{:S(2)}) collective-permute-start(bf16[2,80,1024]{2,1,0:T(8,128)(2,1)S(1)} %constant_dynamic-update-slice_fusion.w0), channel_id=1, source_target_pairs={{0,7},{1,0},{2,1},{3,2},{4,3},{5,4},{6,5},{7,6},{8,15},{9,8},{10,9... | collective-permute-start | bytes 983048 | tf_op jit(solution)/shard_map/ppermute | solution.py:404
  102.6 15.5 %collective-permute-start.5 = (bf16[2,80,1024]{2,1,0:T(8,128)(2,1)S(1)}, bf16[2,80,1024]{2,1,0:T(8,128)(2,1)S(1)}, u32[]{:S(2)}, u32[]{:S(2)}) collective-permute-start(bf16[2,80,1024]{2,1,0:T(8,128)(2,1)S(1)} %constant_dynamic-update-slice_fusion.w0), channel_id=1, source_target_pairs={{0,1},{1,2},{2,3},{3,4},{4,5},{5,6},{6,7},{7,0},{8,9},{9,10},{10,1... | collective-permute-start | bytes 983048 | tf_op jit(solution)/shard_map/ppermute | solution.py:404
  104.5 9.6 %collective-permute-start.2 = (bf16[1,80,1024]{2,1,0:T(8,128)(2,1)S(1)}, bf16[1,80,1024]{2,1,0:T(8,128)(2,1)S(1)}, u32[]{:S(2)}, u32[]{:S(2)}) collective-permute-start(bf16[1,80,1024]{2,1,0:T(8,128)(2,1)S(1)} %bitcast.17), channel_id=1, source_target_pairs={{0,6},{1,7},{2,0},{3,1},{4,2},{5,3},{6,4},{7,5},{8,14},{9,15},{10,... | collective-permute-start | bytes 491528 | tf_op jit(solution)/shard_map/ppermute | solution.py:404
  107.8 10.3 %collective-permute-start.3 = (bf16[1,80,1024]{2,1,0:T(8,128)(2,1)S(1)}, bf16[1,80,1024]{2,1,0:T(8,128)(2,1)S(1)}, u32[]{:S(2)}, u32[]{:S(2)}) collective-permute-start(bf16[1,80,1024]{2,1,0:T(8,128)(2,1)S(1)} %bitcast.18), channel_id=1, source_target_pairs={{0,2},{1,3},{2,4},{3,5},{4,6},{5,7},{6,0},{7,1},{8,10},{9,11},{10,... | collective-permute-start | bytes 491528 | tf_op jit(solution)/shard_map/ppermute | solution.py:404
  152.1 8.0 %collective-permute-start.6 = (bf16[32,8192]{1,0:T(8,128)(2,1)S(1)}, bf16[32,8192]{1,0:T(8,128)(2,1)S(1)}, u32[]{:S(2)}, u32[]{:S(2)}) collective-permute-start(bf16[32,8192]{1,0:T(8,128)(2,1)S(1)} %bitcast.10), channel_id=1, source_target_pairs={{0,8},{8,0},{16,24},{24,16},{32,40},{40,32},{48,56},{56,48},{64,72... | collective-permute-start | bytes 1572872 | tf_op jit(solution)/shard_map/ppermute | solution.py:436

commit v3 on v2

--- a/solution.py
+++ b/solution.py
@@ -14,6 +14,7 @@
 X, Z = 4, 8
 CHIPS = X * Z
 T = 8
+BRANCHES = 4 * CHIPS
 ROWS = CHIPS * 8
 WIDTH = HEADS * HD
 PACKED = WIDTH + 128
@@ -21,8 +22,6 @@
 SCALE = math.log2(math.e) / math.sqrt(HD)
 PROMPT, KEYS = 2048, 4096
 WINDOW = 64
-OFFSETS = (0, 4, 2, 6, 1, 5, 7, 3)
-WEIGHT_AT = ((0, 0), (0, 1), (1, 0), (2, 0), (3, 0), (3, 1), (4, 0), (4, 1))
 NEG = -1e30
 NT = (((1,), (1,)), ((), ()))
 BF16, F32 = jnp.bfloat16, jnp.float32
@@ -38,9 +37,8 @@
 
 
 XZ_GROUPS = [[page_id(x, z, c) for x in range(X) for z in range(Z)] for c in range(2)]
-X_GROUPS = [[page_id(x, z, c) for x in range(X)] for z in range(Z) for c in range(2)]
-ZT_GROUPS = [
-    [page_id(x, z, c) * T + t for z in range(Z) for t in range(T)] for x in range(X) for c in range(2)
+CT_GROUPS = [
+    [page_id(x, z, c) * T + t for c in range(2) for t in range(T)] for x in range(X) for z in range(Z)
 ]
 CORE_SWAP = [(p, p ^ 1) for p in range(2 * CHIPS)]
 
@@ -63,11 +61,12 @@
 
 
 def prep_kernel(
-    chip_ref, groups_ref, lengths_ref, row_group_ref, new_keys_ref, new_values_ref, *refs,
+    page_ref, lengths_ref, branch_group_ref, page_list_ref, new_keys_ref, new_values_ref, *refs,
 ):
-    sources, results, held, made = refs[:7], refs[7:15], refs[15:25], refs[25:33]
-    in_sems, out_sems = refs[33:]
-    sources = sources[:4] + tuple(sources[4].at[n * 1024 : (n + 1) * 1024] for n in range(4)) + sources[5:]
+    sources, results, at_ref, held, made = refs[:8], refs[8:16], refs[16], refs[17:27], refs[27:35]
+    in_sems, out_sems = refs[35:]
+    halves = [each.at[n * 1024 : (n + 1) * 1024] for each in sources[4:6] for n in range(2)]
+    sources = [*sources[:4], *halves, *sources[6:]]
     suffix_keys_ref, suffix_values_ref = held[8:]
     keys_ref, values_ref, own_keys_ref, own_values_ref, longest_ref, sort_ref, unsort_ref, marks_ref = made
     incoming = copies_of(list(zip(sources, held)), in_sems)
@@ -83,16 +82,30 @@
     ones = jnp.ones((PAGE, HD), BF16)
     down = lax.broadcasted_iota(jnp.int32, (ROWS, ROWS), 0)
     across = lax.broadcasted_iota(jnp.int32, (ROWS, ROWS), 1)
-    group_across = row_group_ref[...]
+    page, core, chip = page_ref[0], lax.rem(page_ref[0], 2), lax.div(page_ref[0], 2)
+    branch = lax.broadcasted_iota(jnp.int32, (BRANCHES, ROWS), 0)
+    row = lax.broadcasted_iota(jnp.int32, (BRANCHES, ROWS), 1)
+    its_branch = (branch == 4 * (row // 8) + 2 * core + row % 8 // 4).astype(BF16)
+    branch_group = jnp.broadcast_to(branch_group_ref[...].astype(F32), (8, BRANCHES)).astype(BF16)
+    group_across = jnp.dot(branch_group, its_branch, preferred_element_type=F32)[0:1].astype(jnp.int32)
+    order_across = group_across * ROWS + lax.broadcasted_iota(jnp.int32, (1, ROWS), 1)
+
+    page_list = page_list_ref[...]
+    list_group = lax.broadcasted_iota(jnp.int32, page_list.shape, 0)
+    groups = []
+    for j in range(8):
+        page_id = 4 * (page if j < 4 else page + 1 - 2 * core) + j % 4
+        found = jnp.sum(jnp.where(page_list == page_id, list_group, 0), axis=0, keepdims=True)
+        groups.append(jnp.sum(found, axis=1, keepdims=True))
     group_down = jnp.sum(jnp.where(down == across, group_across, 0), axis=1, keepdims=True)
     before = group_down * ROWS + down < group_across * ROWS + across
     rank = jnp.sum(before.astype(jnp.int32), axis=0, keepdims=True)
     sort = (rank == down).astype(BF16)
     sort_ref[...] = sort
-    order = ((down % 8) * CHIPS + down // 8 == across).astype(BF16)
-    unsort_ref[...] = lax.dot_general(order, sort, NT, preferred_element_type=F32).astype(BF16)
+    same = (down == across).astype(BF16)
+    unsort_ref[...] = lax.dot_general(same, sort, NT, preferred_element_type=F32).astype(BF16)
     mark = lax.broadcasted_iota(jnp.int32, (ROWS, 128), 1)
-    place = lax.broadcasted_iota(jnp.int32, (ROWS, 128), 0) - chip_ref[0] * 8
+    place = lax.broadcasted_iota(jnp.int32, (ROWS, 128), 0) - chip * 8
     own = (place >= 0) & (place < 8)
     marks = (mark == 16 + group_down) | (own & (mark == 32 + place)) | (jnp.logical_not(own) & (mark == 40))
     marks_ref[...] = jnp.dot(sort, marks.astype(BF16), preferred_element_type=F32)
@@ -110,7 +123,7 @@
             longest = jnp.maximum(longest, jnp.sum(wide * wide, axis=1, keepdims=True))
             more = (lane < 8).astype(F32)
             if group_at is not None:
-                hidden = (lane >= 16) & (lane < 32) & (lane != 16 + groups_ref[group_at + j])
+                hidden = (lane >= 16) & (lane < 32) & (lane != 16 + groups[group_at + j])
                 more = jnp.where(hidden, NEG, more)
             keys_ref[rows, :HD] = key
             keys_ref[rows, HD:] = more.astype(BF16)
@@ -151,22 +164,34 @@
     longest_ref[2:8, :] = jnp.zeros((6, 128), F32)
     for copy in outgoing[:3]:
         copy.start()
+    own_row = lax.broadcasted_iota(jnp.int32, (1, ROWS), 1) - chip * 8
+    limits = [group * ROWS for group in groups] + [(group + 1) * ROWS for group in groups]
+    for j in range(2):
+        limits.append(jnp.sum(jnp.where(own_row == 4 * j, order_across, 0), axis=1, keepdims=True))
+    below = [jnp.sum((order_across < limit).astype(jnp.int32), axis=1, keepdims=True) for limit in limits]
+    for j in range(18):
+        at_ref[j] = below[j][0, 0]
     for copy in outgoing:
         copy.wait()
 
 
 def attend_kernel(
-    at_ref, *refs,
+    at_ref, q_ref, *refs,
 ):
     sources, out_ref, (q_rows, shift_ref, total_ref, sent_ref), held, sems = (
-        refs[:9], refs[9], refs[10:14], refs[14:23], refs[23]
-    )
-    keys_ref, values_ref, own_keys_ref, own_values_ref, longest_ref, sort_ref, unsort_ref, marks_ref, q_ref = held
-    copies = copies_of(list(zip(sources, held)), sems)
-    for i in (8, 5, 7, 4, 0, 1, 2, 3, 6):
-        copies[i].start()
-    for i in (8, 5, 7, 4):
-        copies[i].wait()
+        refs[:8], refs[8], refs[9:13], refs[13:21], refs[21]
+    )
+    keys_ref, values_ref, own_keys_ref, own_values_ref, longest_ref, sort_ref, unsort_ref, marks_ref = held
+    first, later = pl.ds(0, PROMPT), pl.ds(PROMPT, KEYS - PROMPT)
+    pairs = list(zip(sources, held))
+    pairs = [pairs[5], pairs[7], pairs[4]] + [
+        (a.at[rows], b.at[rows]) for rows in (first, later) for a, b in pairs[:2]
+    ] + [pairs[2], pairs[3], pairs[6]]
+    copies = copies_of(pairs, sems)
+    for copy in copies:
+        copy.start()
+    for copy in copies[:3]:
+        copy.wait()
     lane = lax.broadcasted_iota(jnp.int32, (ROWS, 128), 1)
     q_all = jnp.dot(sort_ref[...], q_ref[...], preferred_element_type=F32)
     by_head = lax.broadcasted_iota(jnp.int32, (WIDTH, 128), 0) // HD == lax.broadcasted_iota(jnp.int32, (WIDTH, 128), 1)
@@ -193,11 +218,13 @@
     def page(j):
         return pl.ds(pl.multiple_of(PROMPT + j * PAGE, PAGE), PAGE)
 
-    for i in (0, 1, 2, 3, 6):
-        copies[i].wait()
+    for copy in copies[3:5]:
+        copy.wait()
     for h in range(HEADS):
         power = powers(q_rows[h], keys_ref[:PROMPT, :])
         total_ref[h] = jnp.dot(power, values_ref[:PROMPT, :], preferred_element_type=F32)
+    for copy in copies[5:]:
+        copy.wait()
     firsts = [jnp.minimum(lax.div(at_ref[j], 16) * 16, ROWS - WINDOW) for j in range(8)]
     parts = [taken(j, firsts[j], WINDOW, keys_ref[page(j), :], values_ref[page(j), :]) for j in range(8)]
     parts += [
@@ -277,34 +304,26 @@
     weights = jnp.exp2(lse - top)
     weights = weights / jnp.sum(weights, axis=0, keepdims=True)
     for h in range(HEADS):
-        rows = came_ref[:, :, h * HD : (h + 1) * HD].astype(F32)
-        rows_ref[:, h, :] = jnp.sum(rows * weights[:, :, h : h + 1], axis=0)
+        cols = slice(h * HD, (h + 1) * HD)
+        rows_ref[:, cols] = jnp.sum(came_ref[:, :, cols].astype(F32) * weights[:, :, h : h + 1], axis=0)
     rows = rows_ref[...].astype(BF16)
-    for z in range(Z):
-        out_ref[z] = rows
-
-
-def project(rank_ref, rows_ref, weight_refs):
-    total = 0.0
-    for j, offset in enumerate(OFFSETS):
-        block = lax.rem(rank_ref[0] + offset, T)
-        rows = rows_ref[:, pl.ds(pl.multiple_of(block * WIDTH, WIDTH), WIDTH)]
-        ref, at = WEIGHT_AT[j]
-        total = total + lax.dot_general(rows, weight_refs[ref][at], NT, preferred_element_type=F32)
-    return total
-
-
-def project_mine_kernel(rank_ref, rows_ref, w0, w1, w2, w3, w4, out_ref):
-    out_ref[...] = project(rank_ref, rows_ref, (w0, w1, w2, w3, w4))
-
-
-def project_all_kernel(rank_ref, core_ref, rows_ref, w0, w1, w2, w3, w4, mine_ref, out_ref):
-    theirs, mine = project(rank_ref, rows_ref, (w0, w1, w2, w3, w4)), mine_ref[...]
-    even = jnp.where(core_ref[0] == 0, mine, theirs)
-    odd = jnp.where(core_ref[0] == 0, theirs, mine)
-    pieces = []
-    for x in range(X):
-        pieces += [even[x * Z : (x + 1) * Z], odd[x * Z : (x + 1) * Z]]
+    for i in range(CHIPS):
+        out_ref[i] = rows
+
+
+def project_kernel(core_ref, rows_ref, mine_ref, other_ref, out_ref):
+    rows = rows_ref[...]
+    mine = lax.dot_general(rows, mine_ref[...], NT, preferred_element_type=F32)
+    other = lax.dot_general(rows, other_ref[...], NT, preferred_element_type=F32)
+    first = core_ref[0] == 0
+    for c, block in enumerate((jnp.where(first, mine, other), jnp.where(first, other, mine))):
+        for t in range(T):
+            out_ref[c * T + t] = block[t * CHIPS : (t + 1) * CHIPS].astype(BF16)
+
+
+def total_kernel(shares_ref, out_ref):
+    halves = [jnp.sum(shares_ref[c * T : (c + 1) * T].astype(F32), axis=0) for c in range(2)]
+    pieces = [halves[c][i * 8 : (i + 1) * 8] for i in range(CHIPS // 8) for c in range(2)]
     out_ref[...] = jnp.concatenate(pieces, axis=0).astype(BF16)
 
 
@@ -333,9 +352,9 @@
 def prepare(*args):
     return pl.pallas_call(
         prep_kernel,
-        out_shape=[jax.ShapeDtypeStruct(*each) for each in PREPARED],
-        in_specs=[SMEM] * 3 + [VMEM] * 3 + [HBM] * 7,
-        out_specs=[HBM] * 8,
+        out_shape=[jax.ShapeDtypeStruct(*each) for each in PREPARED] + [jax.ShapeDtypeStruct((18,), jnp.int32)],
+        in_specs=[SMEM] * 2 + [VMEM] * 4 + [HBM] * 8,
+        out_specs=[HBM] * 8 + [SMEM],
         scratch_shapes=[pltpu.VMEM((1024, HD), BF16)] * 8
         + [pltpu.VMEM((2, SUFFIX, HD), BF16)] * 2
         + [pltpu.VMEM(*each) for each in PREPARED]
@@ -349,7 +368,7 @@
     return pl.pallas_call(
         attend_kernel,
         out_shape=jax.ShapeDtypeStruct((ROWS, PACKED), BF16),
-        in_specs=[SMEM] + [HBM] * 9,
+        in_specs=[SMEM, VMEM] + [HBM] * 8,
         out_specs=VMEM,
         scratch_shapes=[
             pltpu.VMEM((HEADS, ROWS, 2 * HD), BF16),
@@ -358,8 +377,8 @@
             pltpu.VMEM((ROWS, PACKED), BF16),
         ]
         + [pltpu.VMEM(*each) for each in PREPARED]
-        + [pltpu.VMEM((ROWS, WIDTH), BF16), pltpu.SemaphoreType.DMA((9,))],
-        compiler_params=pltpu.CompilerParams(vmem_limit_bytes=62_800_000),
+        + [pltpu.SemaphoreType.DMA((10,))],
+        compiler_params=PARAMS,
     )(*args)
 
 
@@ -378,77 +397,52 @@
     page_list,
     out_weight,
 ):
-    page, rank = lax.axis_index("page"), lax.axis_index("tensor").reshape(1)
-    core, chip = lax.rem(page, 2), lax.div(page, 2)
+    page = lax.axis_index("page")
+    core = lax.rem(page, 2)
     sent, prompt_keys, pool_keys, prompt_values, pool_values = lax.optimization_barrier(
         (spread(queries), prompt_keys, pool_keys, prompt_values, pool_values)
     )
     gathered = lax.all_to_all(sent, "page", 0, 0, tiled=True, axis_index_groups=XZ_GROUPS)
     gathered = gathered.reshape(ROWS, WIDTH)
-    row_group = lax.dynamic_index_in_dim(branch_group.reshape(CHIPS, 2, 2), core, 1, keepdims=False)
-    row_group = jnp.repeat(row_group.reshape(-1), 4)
-    order = row_group * ROWS + jnp.arange(ROWS)
-    page_ids = jnp.concatenate([page * 4 + jnp.arange(4), (page ^ 1) * 4 + jnp.arange(4)])
-    matched = page_list[:, :, None] == page_ids[None, None, :]
-    page_group = jnp.sum(
-        jnp.where(matched, jnp.arange(page_list.shape[0])[:, None, None], 0), axis=(0, 1)
-    )
-    own_group = lax.dynamic_slice_in_dim(branch_group, 2 * page, 2)
-    limits = jnp.concatenate(
-        [page_group * ROWS, (page_group + 1) * ROWS, own_group * ROWS + chip * 8 + jnp.arange(2) * 4]
-    )
-    at = jnp.sum((order[:, None] < limits[None, :]).astype(jnp.int32), axis=0)
     own_pages = [prompt_keys, prompt_values, pool_keys, pool_values]
-    other_pages = lax.ppermute(jnp.concatenate(own_pages, axis=0), "page", CORE_SWAP)
-    def from_rank(offset, array):
-        return lax.ppermute(array, "tensor", [(t, (t - offset) % T) for t in range(T)])
-
-    weight, other_pages = lax.optimization_barrier((out_weight.T[None], other_pages))
-    across, after, before = from_rank(4, weight), from_rank(2, weight), from_rank(6, weight)
-    prepared = prepare(
-        chip.reshape(1), page_group, suffix_lengths, row_group.reshape(1, ROWS), new_keys, new_values,
-        *own_pages, other_pages, suffix_keys, suffix_values,
-    )
-    gathered, across = lax.optimization_barrier((gathered, across))
-    packed = attend(at, *prepared, gathered)
-    packed, weight = lax.optimization_barrier((packed, weight))
-    two = jnp.concatenate([weight, across], axis=0)
-    next_two, last_two = from_rank(1, two), from_rank(7, two)
-    came_rows = lax.all_to_all(
+    pairs = [jnp.concatenate(pair, axis=0) for pair in ((prompt_keys, prompt_values), (pool_keys, pool_values))]
+    other_pages = [lax.ppermute(pair, "page", CORE_SWAP) for pair in pairs]
+    *prepared, at = prepare(
+        page.reshape(1), suffix_lengths, branch_group.reshape(1, BRANCHES), page_list, new_keys, new_values,
+        *own_pages, *other_pages, suffix_keys, suffix_values,
+    )
+    packed = attend(at, gathered, *prepared)
+    packed, weight = lax.optimization_barrier((packed, out_weight.T))
+    other_weight = lax.ppermute(weight, "page", CORE_SWAP)
+    came = lax.all_to_all(
         packed.reshape(CHIPS, 8, PACKED), "page", 0, 0, tiled=True, axis_index_groups=XZ_GROUPS
     )
-    weights = [two, after, before, next_two, last_two]
-    came_rows, *weights = lax.optimization_barrier((came_rows, *weights))
+    came, other_weight = lax.optimization_barrier((came, other_weight))
     rows = pl.pallas_call(
         merge_kernel,
-        out_shape=jax.ShapeDtypeStruct((Z, T, HEADS, HD), BF16),
+        out_shape=jax.ShapeDtypeStruct((CHIPS, 8, WIDTH), BF16),
         in_specs=[VMEM],
         out_specs=VMEM,
-        scratch_shapes=[pltpu.VMEM((8, HEADS, HD), F32)],
+        scratch_shapes=[pltpu.VMEM((8, WIDTH), F32)],
         compiler_params=SMALL,
-    )(came_rows)
-    rows = lax.all_to_all(
-        rows.reshape(Z * T, HEADS, HD), ("page", "tensor"), 0, 0, tiled=True, axis_index_groups=ZT_GROUPS
-    )
-    rows = jnp.broadcast_to(rows.reshape(1, Z, T * WIDTH), (X, Z, T * WIDTH))
-    rows = lax.all_to_all(rows, "page", 0, 0, tiled=True, axis_index_groups=X_GROUPS)
-    rows = rows.reshape(CHIPS, T * WIDTH)
-    rows_other = lax.ppermute(rows, "page", CORE_SWAP)
+    )(came)
+    rows = lax.all_to_all(rows, "page", 0, 0, tiled=True, axis_index_groups=XZ_GROUPS)
     columns = out_weight.shape[1]
-    mine = pl.pallas_call(
-        project_mine_kernel,
-        out_shape=jax.ShapeDtypeStruct((CHIPS, columns), F32),
-        in_specs=[SMEM] + [VMEM] * 6,
+    shares = pl.pallas_call(
+        project_kernel,
+        out_shape=jax.ShapeDtypeStruct((2 * T, CHIPS, columns), BF16),
+        in_specs=[SMEM] + [VMEM] * 3,
         out_specs=VMEM,
         compiler_params=SMALL,
-    )(rank, rows, *weights)
+    )(core.reshape(1), rows.reshape(ROWS, WIDTH), weight, other_weight)
+    shares = lax.all_to_all(shares, ("page", "tensor"), 0, 0, tiled=True, axis_index_groups=CT_GROUPS)
     return pl.pallas_call(
-        project_all_kernel,
+        total_kernel,
         out_shape=jax.ShapeDtypeStruct((2 * CHIPS, columns), BF16),
-        in_specs=[SMEM] * 2 + [VMEM] * 7,
+        in_specs=[VMEM],
         out_specs=VMEM,
         compiler_params=SMALL,
-    )(rank, core.reshape(1), rows_other, *weights, mine)
+    )(shares)
 
 
 def solution(mesh):

time: 162 us -> 151 us (0.932)
  waiting for transfers between devices: 8.55 us -> 28.4 us
  blocking collectives: 33.4 us -> 18 us
  starting transfers between devices: 52.6 us -> 38.8 us
    ppermute x7 -> x3, starting transfers between devices: 36.6 us -> 7.55 us  [the longest x2 4.78 us: local(): other_pages = [lax.ppermute(pair, 'page', CORE_SWAP) for pair in pairs]]
    all_to_all x2 -> x1, blocking collectives: 33.4 us -> 18 us  [local(): lax.all_to_all(shares, ('page', 'tensor'), 0, 0, tiled=True, axis_index_g...]
    all_to_all x0 -> x1, waiting for transfers between devices: none -> 13.8 us  [local(): lax.all_to_all(rows, 'page', 0, 0, tiled=True, axis_index_groups=XZ_GROUPS)]
    all_to_all x1, waiting for transfers between devices: 0.01 us -> 11.5 us  [local(): lax.all_to_all(packed.reshape(CHIPS, 8, PACKED), 'page', 0, 0, tiled=True...]
    all_to_all x0 -> x1, starting transfers between devices: none -> 8.15 us  [local(): lax.all_to_all(rows, 'page', 0, 0, tiled=True, axis_index_groups=XZ_GROUPS)]
    all_to_all x1, starting transfers between devices: 7.53 us -> 13.7 us  [local(): lax.all_to_all(sent, 'page', 0, 0, tiled=True, axis_index_groups=XZ_GROUPS)]
    ppermute x7 -> x3, waiting for transfers between devices: 8.45 us -> 2.86 us  [the longest x2 1.85 us: local(): other_pages = [lax.ppermute(pair, 'page', CORE_SWAP) for pair in pairs]]
  transfers between devices with their start and end apart: 9 -> 6, of which waited for: 4 -> 5; matrix products, arithmetic and copies ran while one was open for 2% -> 1% of each run, Pallas kernels for 3% -> 4%
where the time goes in v3:
time: 151 us
  Pallas kernels  62.5 us (41%)
  starting transfers between devices  38.8 us (26%)
  waiting for transfers between devices  28.4 us (19%)
  blocking collectives  18 us (12%)
  local copies, waits for them, and re-layouts  1.62 us (1%)
    pallas_call x1, Pallas kernels, attend(): pl.pallas_call(attend_kernel, out_shape=jax.ShapeDtypeStruct((ROWS, PACKE...  53 us
    all_to_all x1, blocking collectives, local(): lax.all_to_all(shares, ('page', 'tensor'), 0, 0, tiled=True, axis_index_g...  18 us
    all_to_all x1, waiting for transfers between devices, local(): lax.all_to_all(rows, 'page', 0, 0, tiled=True, axis_index_groups=XZ_GROUPS)  13.8 us
    all_to_all x1, starting transfers between devices, local(): lax.all_to_all(sent, 'page', 0, 0, tiled=True, axis_index_groups=XZ_GROUPS)  13.7 us
    all_to_all x1, waiting for transfers between devices, local(): lax.all_to_all(packed.reshape(CHIPS, 8, PACKED), 'page', 0, 0, tiled=True...  11.5 us
    all_to_all x1, starting transfers between devices, local(): lax.all_to_all(packed.reshape(CHIPS, 8, PACKED), 'page', 0, 0, tiled=True...  9.35 us
    all_to_all x1, starting transfers between devices, local(): lax.all_to_all(rows, 'page', 0, 0, tiled=True, axis_index_groups=XZ_GROUPS)  8.15 us
    pallas_call x1, Pallas kernels, prepare(): pl.pallas_call(prep_kernel, out_shape=[jax.ShapeDtypeStruct(*each) for ea...  5.49 us
  transfers between devices with their start and end apart: 6, of which 5 were waited for; matrix products, arithmetic and copies ran while one was open for 1% of the time, Pallas kernels for 4%

profile of v3, /device:TPU:1, one launch (start us, length us, event | category | flops | bytes accessed | tf_op | source)
XLA Modules:
  0.0 150.5 jit_solution(3971174014383461717)
XLA Ops:
  0.0 0.0 copy-start.2
  0.0 0.0 copy-start.3
  0.0 1.6 %shard_map.127 = bf16[32,8,1024]{2,1,0:T(8,128)(2,1)} custom-call(bf16[2,4,1024]{2,1,0:T(4,128)(2,1)} %q_ref.1), custom_call_target="tpu_custom_call" | custom-call | tf_op jit(solution)/shard_map/pallas_call | solution.py:331
  1.6 13.7 %all-to-all-start = ((bf16[32,8,1024]{2,1,0:T(8,128)(2,1)}), bf16[32,8,1024]{2,1,0:T(8,128)(2,1)S(1)}, u32[]{:S(2)}, u32[]{:S(2)}) async-start(bf16[32,8,1024]{2,1,0:T(8,128)(2,1)} %shard_map.127), calls=%async_computation | async-start | bytes 1048576 | tf_op jit(solution)/shard_map/all_to_all | solution.py:405
  15.4 1.1 pad_maximum_fusion.1
  16.4 2.9 %collective-permute-start.1 = (bf16[2048,128]{1,0:T(8,128)(2,1)S(1)}, bf16[2048,128]{1,0:T(8,128)(2,1)S(1)}, u32[]{:S(2)}, u32[]{:S(2)}) collective-permute-start(bf16[2048,128]{1,0:T(8,128)(2,1)S(1)} %pad_maximum_fusion.1), channel_id=1, source_target_pairs={{0,8},{8,0},{16,24},{24,16},{32,40},{40,32},{48,56},{56,48},{64,72... | collective-permute-start | bytes 1572872 | tf_op jit(solution)/shard_map/ppermute | solution.py:409
  19.3 0.0 copy-done.2
  19.3 0.0 copy-done.3
  19.4 1.9 %collective-permute-start = (bf16[2048,128]{1,0:T(8,128)(2,1)S(1)}, bf16[2048,128]{1,0:T(8,128)(2,1)S(1)}, u32[]{:S(2)}, u32[]{:S(2)}) collective-permute-start(bf16[2048,128]{1,0:T(8,128)(2,1)S(1)} %pad_maximum_fusion), channel_id=1, source_target_pairs={{0,8},{8,0},{16,24},{24,16},{32,40},{40,32},{48,56},{56,48},{64,72... | collective-permute-start | bytes 1572872 | tf_op jit(solution)/shard_map/ppermute | solution.py:409
  21.3 0.0 collective-permute-done.1.refs_5_
  21.3 0.0 copy-start.4
  21.3 1.9 %collective-permute-done.refs_4_ = bf16[2048,128]{1,0:T(8,128)(2,1)S(1)} collective-permute-done((bf16[2048,128]{1,0:T(8,128)(2,1)S(1)}, bf16[2048,128]{1,0:T(8,128)(2,1)S(1)}, u32[]{:S(2)}, u32[]{:S(2)}) %collective-permute-start) | collective-permute-done | bytes 524320 | tf_op jit(solution)/shard_map/ppermute | solution.py:409
  23.2 0.0 copy-start.5
  23.2 0.0 copy-done.4
  23.2 0.8 copy-done.5
  24.0 5.5 %shard_map.128 = (bf16[4096,256]{1,0:T(8,128)(2,1)}, bf16[4096,256]{1,0:T(8,128)(2,1)}, bf16[2,528,256]{2,1,0:T(8,128)(2,1)}, bf16[2,528,256]{2,1,0:T(8,128)(2,1...) custom-call(s32[1]{0:T(128)} %bitcast.1.page_ref, ...), custom_call_target="tpu_custom_call" | custom-call | flops 1 | bytes 1 | tf_op jit(solution)/shard_map/pallas_call | solution.py:353
  29.5 0.2 all-to-all-done
  29.7 0.0 copy-start.1
  29.7 0.8 copy-done.1
  30.5 0.0 copy-start
  30.5 53.0 %shard_map.129 = bf16[256,1152]{1,0:T(8,128)(2,1)} custom-call(s32[18]{0:T(128)} %get-tuple-element.27.at_ref, bf16[256,1024]{1,0:T(8,128)(2,1)} %bitcast.11, bf16[4096,256]{1,0:T(8,128)(2,1)} %get-tuple-element.29.refs_0_, bf16[4096,256]{1,0:T(8,128)(2,1)} %get-tuple-element.30.refs_1_, bf16[2,528,256]{2,1,0:T(8,128)(2,1)} %get-tuple-element.31.refs_2_, ...), custom_call_target="tpu_custom_call" | custom-call | tf_op jit(solution)/shard_map/pallas_call | solution.py:368
  83.5 9.3 %all-to-all-start.1 = ((bf16[32,8,1152]{2,1,0:T(8,128)(2,1)}), bf16[32,8,1152]{2,1,0:T(8,128)(2,1)S(1)}, u32[]{:S(2)}, u32[]{:S(2)}) async-start(bf16[32,8,1152]{2,1,0:T(8,128)(2,1)} %bitcast.10), calls=%async_computation.1 | async-start | bytes 1179648 | tf_op jit(solution)/shard_map/all_to_all | solution.py:417
  92.8 0.0 copy-done
  92.8 2.8 %collective-permute-start.2 = (bf16[80,1024]{1,0:T(8,128)(2,1)S(1)}, bf16[80,1024]{1,0:T(8,128)(2,1)S(1)}, u32[]{:S(2)}, u32[]{:S(2)}) collective-permute-start(bf16[80,1024]{1,0:T(8,128)(2,1)S(1)} %bitcast.8), channel_id=1, source_target_pairs={{0,8},{8,0},{16,24},{24,16},{32,40},{40,32},{48,56},{56,48},{64,72... | collective-permute-start | bytes 491528 | tf_op jit(solution)/shard_map/ppermute | solution.py:416
  95.6 1.0 collective-permute-done.2.other_ref
  96.6 11.5 %all-to-all-done.1.came_ref = bf16[32,8,1152]{2,1,0:T(8,128)(2,1)S(1)} async-done(((bf16[32,8,1152]{2,1,0:T(8,128)(2,1)}), bf16[32,8,1152]{2,1,0:T(8,128)(2,1)S(1)}, u32[]{:S(2)}, u32[]{:S(2)}) %all-to-all-start.1) | async-done | bytes 589856 | tf_op jit(solution)/shard_map/all_to_all | solution.py:417
  108.1 1.3 shard_map.130
  109.4 8.2 %all-to-all-start.2 = ((bf16[32,8,1024]{2,1,0:T(8,128)(2,1)}), bf16[32,8,1024]{2,1,0:T(8,128)(2,1)S(1)}, u32[]{:S(2)}, u32[]{:S(2)}) async-start(bf16[32,8,1024]{2,1,0:T(8,128)(2,1)} %shard_map.130), calls=%async_computation.2 | async-start | bytes 1048576 | tf_op jit(solution)/shard_map/all_to_all | solution.py:429
  117.6 13.8 %all-to-all-done.2 = bf16[32,8,1024]{2,1,0:T(8,128)(2,1)S(1)} async-done(((bf16[32,8,1024]{2,1,0:T(8,128)(2,1)}), bf16[32,8,1024]{2,1,0:T(8,128)(2,1)S(1)}, u32[]{:S(2)}, u32[]{:S(2)}) %all-to-all-start.2) | async-done | bytes 524320 | tf_op jit(solution)/shard_map/all_to_all | solution.py:429
  131.4 0.4 shard_map.131
  131.8 18.0 %all_to_all.20.shares_ref = bf16[16,32,80]{2,1,0:T(8,128)(2,1)S(1)} all-to-all(bf16[16,32,80]{2,1,0:T(8,128)(2,1)S(1)} %shard_map.131), channel_id=1, replica_groups={{0,1,2,3,4,5,6,7,8,9,10,11,12,13,14,15},{16,17,18,19,20,21,22,23,24,25,..., dimensions={0} | all-to-all | bytes 163840 | tf_op jit(solution)/shard_map/all_to_all | solution.py:438
  149.9 0.6 shard_map.132
  (1 shorter events, 0.0 us)
Async XLA Ops:
  0.0 19.3 %copy-start.2 = (bf16[1024,128]{1,0:T(8,128)(2,1)S(1)}, bf16[1024,128]{1,0:T(8,128)(2,1)}, u32[]{:S(2)}) copy-start(bf16[1024,128]{1,0:T(8,128)(2,1)} %refs_0_) | copy-start | bytes 786436
  0.0 19.3 %copy-start.3 = (bf16[1024,128]{1,0:T(8,128)(2,1)S(1)}, bf16[1024,128]{1,0:T(8,128)(2,1)}, u32[]{:S(2)}) copy-start(bf16[1024,128]{1,0:T(8,128)(2,1)} %refs_1_) | copy-start | bytes 786436
  1.6 28.0 %all-to-all-start = ((bf16[32,8,1024]{2,1,0:T(8,128)(2,1)}), bf16[32,8,1024]{2,1,0:T(8,128)(2,1)S(1)}, u32[]{:S(2)}, u32[]{:S(2)}) async-start(bf16[32,8,1024]{2,1,0:T(8,128)(2,1)} %shard_map.127), calls=%async_computation | async-start | bytes 1048576 | tf_op jit(solution)/shard_map/all_to_all | solution.py:405
  16.4 4.9 %collective-permute-start.1 = (bf16[2048,128]{1,0:T(8,128)(2,1)S(1)}, bf16[2048,128]{1,0:T(8,128)(2,1)S(1)}, u32[]{:S(2)}, u32[]{:S(2)}) collective-permute-start(bf16[2048,128]{1,0:T(8,128)(2,1)S(1)} %pad_maximum_fusion.1), channel_id=1, source_target_pairs={{0,8},{8,0},{16,24},{24,16},{32,40},{40,32},{48,56},{56,48},{64,72... | collective-permute-start | bytes 1572872 | tf_op jit(solution)/shard_map/ppermute | solution.py:409
  19.4 3.8 %collective-permute-start = (bf16[2048,128]{1,0:T(8,128)(2,1)S(1)}, bf16[2048,128]{1,0:T(8,128)(2,1)S(1)}, u32[]{:S(2)}, u32[]{:S(2)}) collective-permute-start(bf16[2048,128]{1,0:T(8,128)(2,1)S(1)} %pad_maximum_fusion), channel_id=1, source_target_pairs={{0,8},{8,0},{16,24},{24,16},{32,40},{40,32},{48,56},{56,48},{64,72... | collective-permute-start | bytes 1572872 | tf_op jit(solution)/shard_map/ppermute | solution.py:409
  21.3 1.9 %copy-start.4 = (bf16[2048,128]{1,0:T(8,128)(2,1)}, bf16[2048,128]{1,0:T(8,128)(2,1)S(1)}, u32[]{:S(2)}) copy-start(bf16[2048,128]{1,0:T(8,128)(2,1)S(1)} %collective-permute-done.1.refs_5_) | copy-start | bytes 1572868
  23.2 0.8 copy-start.5
  29.7 0.8 copy-start.1
  30.5 62.3 %copy-start = (bf16[1024,80]{0,1:T(8,128)(2,1)S(1)}, bf16[1024,80]{0,1:T(8,128)(2,1)}, u32[]{:S(2)}) copy-start(bf16[1024,80]{0,1:T(8,128)(2,1)} %param.25) | copy-start | bytes 491524
  83.5 24.7 %all-to-all-start.1 = ((bf16[32,8,1152]{2,1,0:T(8,128)(2,1)}), bf16[32,8,1152]{2,1,0:T(8,128)(2,1)S(1)}, u32[]{:S(2)}, u32[]{:S(2)}) async-start(bf16[32,8,1152]{2,1,0:T(8,128)(2,1)} %bitcast.10), calls=%async_computation.1 | async-start | bytes 1179648 | tf_op jit(solution)/shard_map/all_to_all | solution.py:417
  92.8 3.8 %collective-permute-start.2 = (bf16[80,1024]{1,0:T(8,128)(2,1)S(1)}, bf16[80,1024]{1,0:T(8,128)(2,1)S(1)}, u32[]{:S(2)}, u32[]{:S(2)}) collective-permute-start(bf16[80,1024]{1,0:T(8,128)(2,1)S(1)} %bitcast.8), channel_id=1, source_target_pairs={{0,8},{8,0},{16,24},{24,16},{32,40},{40,32},{48,56},{56,48},{64,72... | collective-permute-start | bytes 491528 | tf_op jit(solution)/shard_map/ppermute | solution.py:416
  109.4 22.0 %all-to-all-start.2 = ((bf16[32,8,1024]{2,1,0:T(8,128)(2,1)}), bf16[32,8,1024]{2,1,0:T(8,128)(2,1)S(1)}, u32[]{:S(2)}, u32[]{:S(2)}) async-start(bf16[32,8,1024]{2,1,0:T(8,128)(2,1)} %shard_map.130), calls=%async_computation.2 | async-start | bytes 1048576 | tf_op jit(solution)/shard_map/all_to_all | solution.py:429

commit v4 on v3

--- a/solution.py
+++ b/solution.py
@@ -176,21 +176,21 @@
 
 
 def attend_kernel(
-    at_ref, q_ref, *refs,
+    at_ref, *refs,
 ):
     sources, out_ref, (q_rows, shift_ref, total_ref, sent_ref), held, sems = (
-        refs[:8], refs[8], refs[9:13], refs[13:21], refs[21]
-    )
-    keys_ref, values_ref, own_keys_ref, own_values_ref, longest_ref, sort_ref, unsort_ref, marks_ref = held
+        refs[:9], refs[9], refs[10:14], refs[14:23], refs[23]
+    )
+    q_ref, keys_ref, values_ref, own_keys_ref, own_values_ref, longest_ref, sort_ref, unsort_ref, marks_ref = held
     first, later = pl.ds(0, PROMPT), pl.ds(PROMPT, KEYS - PROMPT)
     pairs = list(zip(sources, held))
-    pairs = [pairs[5], pairs[7], pairs[4]] + [
-        (a.at[rows], b.at[rows]) for rows in (first, later) for a, b in pairs[:2]
-    ] + [pairs[2], pairs[3], pairs[6]]
+    pairs = [pairs[0], pairs[6], pairs[8], pairs[5]] + [
+        (a.at[rows], b.at[rows]) for rows in (first, later) for a, b in pairs[1:3]
+    ] + [pairs[3], pairs[4], pairs[7]]
     copies = copies_of(pairs, sems)
     for copy in copies:
         copy.start()
-    for copy in copies[:3]:
+    for copy in copies[:4]:
         copy.wait()
     lane = lax.broadcasted_iota(jnp.int32, (ROWS, 128), 1)
     q_all = jnp.dot(sort_ref[...], q_ref[...], preferred_element_type=F32)
@@ -218,12 +218,12 @@
     def page(j):
         return pl.ds(pl.multiple_of(PROMPT + j * PAGE, PAGE), PAGE)
 
-    for copy in copies[3:5]:
+    for copy in copies[4:6]:
         copy.wait()
     for h in range(HEADS):
         power = powers(q_rows[h], keys_ref[:PROMPT, :])
         total_ref[h] = jnp.dot(power, values_ref[:PROMPT, :], preferred_element_type=F32)
-    for copy in copies[5:]:
+    for copy in copies[6:]:
         copy.wait()
     firsts = [jnp.minimum(lax.div(at_ref[j], 16) * 16, ROWS - WINDOW) for j in range(8)]
     parts = [taken(j, firsts[j], WINDOW, keys_ref[page(j), :], values_ref[page(j), :]) for j in range(8)]
@@ -311,11 +311,11 @@
         out_ref[i] = rows
 
 
-def project_kernel(core_ref, rows_ref, mine_ref, other_ref, out_ref):
+def project_kernel(page_ref, rows_ref, mine_ref, other_ref, out_ref):
     rows = rows_ref[...]
     mine = lax.dot_general(rows, mine_ref[...], NT, preferred_element_type=F32)
     other = lax.dot_general(rows, other_ref[...], NT, preferred_element_type=F32)
-    first = core_ref[0] == 0
+    first = lax.rem(page_ref[0], 2) == 0
     for c, block in enumerate((jnp.where(first, mine, other), jnp.where(first, other, mine))):
         for t in range(T):
             out_ref[c * T + t] = block[t * CHIPS : (t + 1) * CHIPS].astype(BF16)
@@ -368,7 +368,7 @@
     return pl.pallas_call(
         attend_kernel,
         out_shape=jax.ShapeDtypeStruct((ROWS, PACKED), BF16),
-        in_specs=[SMEM, VMEM] + [HBM] * 8,
+        in_specs=[SMEM] + [HBM] * 9,
         out_specs=VMEM,
         scratch_shapes=[
             pltpu.VMEM((HEADS, ROWS, 2 * HD), BF16),
@@ -376,8 +376,9 @@
             pltpu.VMEM((HEADS, ROWS, 2 * HD), F32),
             pltpu.VMEM((ROWS, PACKED), BF16),
         ]
+        + [pltpu.VMEM((ROWS, WIDTH), BF16)]
         + [pltpu.VMEM(*each) for each in PREPARED]
-        + [pltpu.SemaphoreType.DMA((10,))],
+        + [pltpu.SemaphoreType.DMA((11,))],
         compiler_params=PARAMS,
     )(*args)
 
@@ -398,7 +399,6 @@
     out_weight,
 ):
     page = lax.axis_index("page")
-    core = lax.rem(page, 2)
     sent, prompt_keys, pool_keys, prompt_values, pool_values = lax.optimization_barrier(
         (spread(queries), prompt_keys, pool_keys, prompt_values, pool_values)
     )
@@ -411,13 +411,13 @@
         page.reshape(1), suffix_lengths, branch_group.reshape(1, BRANCHES), page_list, new_keys, new_values,
         *own_pages, *other_pages, suffix_keys, suffix_values,
     )
+    weight = out_weight.T
+    other_weight = lax.ppermute(weight, "page", CORE_SWAP)
+    gathered, other_weight = lax.optimization_barrier((gathered, other_weight))
     packed = attend(at, gathered, *prepared)
-    packed, weight = lax.optimization_barrier((packed, out_weight.T))
-    other_weight = lax.ppermute(weight, "page", CORE_SWAP)
     came = lax.all_to_all(
         packed.reshape(CHIPS, 8, PACKED), "page", 0, 0, tiled=True, axis_index_groups=XZ_GROUPS
     )
-    came, other_weight = lax.optimization_barrier((came, other_weight))
     rows = pl.pallas_call(
         merge_kernel,
         out_shape=jax.ShapeDtypeStruct((CHIPS, 8, WIDTH), BF16),
@@ -434,7 +434,7 @@
         in_specs=[SMEM] + [VMEM] * 3,
         out_specs=VMEM,
         compiler_params=SMALL,
-    )(core.reshape(1), rows.reshape(ROWS, WIDTH), weight, other_weight)
+    )(page.reshape(1), rows.reshape(ROWS, WIDTH), weight, other_weight)
     shares = lax.all_to_all(shares, ("page", "tensor"), 0, 0, tiled=True, axis_index_groups=CT_GROUPS)
     return pl.pallas_call(
         total_kernel,

time: 151 us -> 151 us (level)
  blocking collectives: 18 us -> 65.5 us
  waiting for transfers between devices: 28.4 us -> 0.01 us
  starting transfers between devices: 38.8 us -> 20.9 us
    all_to_all x0 -> x2, blocking collectives: none -> 47.1 us  [the longest x1 26.9 us: local(): lax.all_to_all(packed.reshape(CHIPS, 8, PACKED), 'page', 0, 0, tiled=True...]
    all_to_all x2 -> x0, waiting for transfers between devices: 25.3 us -> none  [the longest x1 13.8 us: local(): lax.all_to_all(rows, 'page', 0, 0, tiled=True, axis_index_groups=XZ_GROUPS)]
    all_to_all x2 -> x0, starting transfers between devices: 17.5 us -> none  [the longest x1 9.35 us: local(): lax.all_to_all(packed.reshape(CHIPS, 8, PACKED), 'page', 0, 0, tiled=True...]
    ppermute x2, waiting for transfers between devices: 1.85 us -> 0.01 us  [local(): other_pages = [lax.ppermute(pair, 'page', CORE_SWAP) for pair in pairs]]
  transfers between devices with their start and end apart: 6 -> 4, of which waited for: 5 -> 0; matrix products, arithmetic and copies ran while one was open for 1% -> 1% of each run, Pallas kernels for 4% -> 4%
where the time goes in v4:
time: 151 us
  blocking collectives  65.5 us (43%)
  Pallas kernels  61.4 us (41%)
  starting transfers between devices  20.9 us (14%)
  local copies, waits for them, and re-layouts  1.79 us (1%)
    pallas_call x1, Pallas kernels, attend(): pl.pallas_call(attend_kernel, out_shape=jax.ShapeDtypeStruct((ROWS, PACKE...  52.7 us
    all_to_all x1, blocking collectives, local(): lax.all_to_all(packed.reshape(CHIPS, 8, PACKED), 'page', 0, 0, tiled=True...  26.9 us
    all_to_all x1, blocking collectives, local(): lax.all_to_all(rows, 'page', 0, 0, tiled=True, axis_index_groups=XZ_GROUPS)  20.2 us
    all_to_all x1, blocking collectives, local(): lax.all_to_all(shares, ('page', 'tensor'), 0, 0, tiled=True, axis_index_g...  18.4 us
    all_to_all x1, starting transfers between devices, local(): lax.all_to_all(sent, 'page', 0, 0, tiled=True, axis_index_groups=XZ_GROUPS)  13.7 us
    pallas_call x1, Pallas kernels, prepare(): pl.pallas_call(prep_kernel, out_shape=[jax.ShapeDtypeStruct(*each) for ea...  5.51 us
    ppermute x2, starting transfers between devices, local(): other_pages = [lax.ppermute(pair, 'page', CORE_SWAP) for pair in pairs]  4.78 us
  transfers between devices with their start and end apart: 4, of which 0 were waited for; matrix products, arithmetic and copies ran while one was open for 1% of the time, Pallas kernels for 4%

profile of v4, /device:TPU:1, one launch (start us, length us, event | category | flops | bytes accessed | tf_op | source)
XLA Modules:
  0.0 150.9 jit_solution(7832146853742045783)
XLA Ops:
  0.0 0.0 copy-start.2
  0.0 0.0 copy-start.3
  0.0 0.0 copy-start
  0.0 1.7 %shard_map.127 = bf16[32,8,1024]{2,1,0:T(8,128)(2,1)} custom-call(bf16[2,4,1024]{2,1,0:T(4,128)(2,1)} %q_ref.1), custom_call_target="tpu_custom_call" | custom-call | tf_op jit(solution)/shard_map/pallas_call | solution.py:331
  1.7 13.7 %all-to-all-start = ((bf16[32,8,1024]{2,1,0:T(8,128)(2,1)}), bf16[32,8,1024]{2,1,0:T(8,128)(2,1)S(1)}, u32[]{:S(2)}, u32[]{:S(2)}) async-start(bf16[32,8,1024]{2,1,0:T(8,128)(2,1)} %shard_map.127), calls=%async_computation | async-start | bytes 1048576 | tf_op jit(solution)/shard_map/all_to_all | solution.py:405
  15.4 1.1 pad_maximum_fusion.1
  16.5 2.9 %collective-permute-start.1 = (bf16[2048,128]{1,0:T(8,128)(2,1)S(1)}, bf16[2048,128]{1,0:T(8,128)(2,1)S(1)}, u32[]{:S(2)}, u32[]{:S(2)}) collective-permute-start(bf16[2048,128]{1,0:T(8,128)(2,1)S(1)} %pad_maximum_fusion.1), channel_id=1, source_target_pairs={{0,8},{8,0},{16,24},{24,16},{32,40},{40,32},{48,56},{56,48},{64,72... | collective-permute-start | bytes 1572872 | tf_op jit(solution)/shard_map/ppermute | solution.py:409
  19.3 0.0 copy-done.2
  19.3 0.0 copy-done.3
  19.4 1.9 %collective-permute-start = (bf16[2048,128]{1,0:T(8,128)(2,1)S(1)}, bf16[2048,128]{1,0:T(8,128)(2,1)S(1)}, u32[]{:S(2)}, u32[]{:S(2)}) collective-permute-start(bf16[2048,128]{1,0:T(8,128)(2,1)S(1)} %pad_maximum_fusion), channel_id=1, source_target_pairs={{0,8},{8,0},{16,24},{24,16},{32,40},{40,32},{48,56},{56,48},{64,72... | collective-permute-start | bytes 1572872 | tf_op jit(solution)/shard_map/ppermute | solution.py:409
  21.3 0.0 copy-done
  21.3 2.4 %collective-permute-start.2 = (bf16[80,1024]{1,0:T(8,128)(2,1)S(1)}, bf16[80,1024]{1,0:T(8,128)(2,1)S(1)}, u32[]{:S(2)}, u32[]{:S(2)}) collective-permute-start(bf16[80,1024]{1,0:T(8,128)(2,1)S(1)} %bitcast.7), channel_id=1, source_target_pairs={{0,8},{8,0},{16,24},{24,16},{32,40},{40,32},{48,56},{56,48},{64,72... | collective-permute-start | bytes 491528 | tf_op jit(solution)/shard_map/ppermute | solution.py:415
  23.7 0.0 collective-permute-done.1.refs_5_
  23.8 0.0 copy-start.4
  23.8 0.0 collective-permute-done.refs_4_
  23.8 0.0 copy-start.5
  23.8 0.8 copy-done.4
  24.6 0.2 copy-done.5
  24.8 5.5 %shard_map.128 = (bf16[4096,256]{1,0:T(8,128)(2,1)}, bf16[4096,256]{1,0:T(8,128)(2,1)}, bf16[2,528,256]{2,1,0:T(8,128)(2,1)}, bf16[2,528,256]{2,1,0:T(8,128)(2,1...) custom-call(s32[1]{0:T(128)} %bitcast.page_ref, ...), custom_call_target="tpu_custom_call" | custom-call | flops 1 | bytes 1 | tf_op jit(solution)/shard_map/pallas_call | solution.py:353
  30.3 0.0 collective-permute-done.2.other_ref
  30.3 0.0 all-to-all-done
  30.3 0.0 copy-start.1
  30.3 0.8 copy-done.1
  31.1 52.7 %shard_map.129 = bf16[256,1152]{1,0:T(8,128)(2,1)} custom-call(s32[18]{0:T(128)} %get-tuple-element.25.at_ref, bf16[256,1024]{1,0:T(8,128)(2,1)} %bitcast.10, bf16[4096,256]{1,0:T(8,128)(2,1)} %get-tuple-element.28.refs_1_, bf16[4096,256]{1,0:T(8,128)(2,1)} %get-tuple-element.29.refs_2_, bf16[2,528,256]{2,1,0:T(8,128)(2,1)} %get-tuple-element.30.refs_3_, ...), custom_call_target="tpu_custom_call" | custom-call | tf_op jit(solution)/shard_map/pallas_call | solution.py:368
  83.8 26.9 %all_to_all.20.came_ref = bf16[32,8,1152]{2,1,0:T(8,128)(2,1)S(1)} all-to-all(bf16[32,8,1152]{2,1,0:T(8,128)(2,1)} %bitcast.9), channel_id=1, replica_groups={{0,16,32,48,64,80,96,112,128,144,160,176,192,208,224,240,256,272,288,30..., dimensions={0} | all-to-all | bytes 1179648 | tf_op jit(solution)/shard_map/all_to_all | solution.py:418
  110.7 0.5 shard_map.130
  111.3 20.2 %all_to_all.21 = bf16[32,8,1024]{2,1,0:T(8,128)(2,1)S(1)} all-to-all(bf16[32,8,1024]{2,1,0:T(8,128)(2,1)S(1)} %shard_map.130), channel_id=1, replica_groups={{0,16,32,48,64,80,96,112,128,144,160,176,192,208,224,240,256,272,288,30..., dimensions={0} | all-to-all | bytes 1048576 | tf_op jit(solution)/shard_map/all_to_all | solution.py:429
  131.5 0.4 shard_map.131
  131.9 18.4 %all_to_all.22.shares_ref = bf16[16,32,80]{2,1,0:T(8,128)(2,1)S(1)} all-to-all(bf16[16,32,80]{2,1,0:T(8,128)(2,1)S(1)} %shard_map.131), channel_id=1, replica_groups={{0,1,2,3,4,5,6,7,8,9,10,11,12,13,14,15},{16,17,18,19,20,21,22,23,24,25,..., dimensions={0} | all-to-all | bytes 163840 | tf_op jit(solution)/shard_map/all_to_all | solution.py:438
  150.3 0.6 shard_map.132
  (1 shorter events, 0.0 us)
Async XLA Ops:
  0.0 19.3 %copy-start.2 = (bf16[1024,128]{1,0:T(8,128)(2,1)S(1)}, bf16[1024,128]{1,0:T(8,128)(2,1)}, u32[]{:S(2)}) copy-start(bf16[1024,128]{1,0:T(8,128)(2,1)} %refs_0_) | copy-start | bytes 786436
  0.0 19.3 %copy-start.3 = (bf16[1024,128]{1,0:T(8,128)(2,1)S(1)}, bf16[1024,128]{1,0:T(8,128)(2,1)}, u32[]{:S(2)}) copy-start(bf16[1024,128]{1,0:T(8,128)(2,1)} %refs_1_) | copy-start | bytes 786436
  0.0 21.3 %copy-start = (bf16[1024,80]{0,1:T(8,128)(2,1)S(1)}, bf16[1024,80]{0,1:T(8,128)(2,1)}, u32[]{:S(2)}) copy-start(bf16[1024,80]{0,1:T(8,128)(2,1)} %param.25) | copy-start | bytes 491524
  1.7 28.6 %all-to-all-start = ((bf16[32,8,1024]{2,1,0:T(8,128)(2,1)}), bf16[32,8,1024]{2,1,0:T(8,128)(2,1)S(1)}, u32[]{:S(2)}, u32[]{:S(2)}) async-start(bf16[32,8,1024]{2,1,0:T(8,128)(2,1)} %shard_map.127), calls=%async_computation | async-start | bytes 1048576 | tf_op jit(solution)/shard_map/all_to_all | solution.py:405
  16.5 7.3 %collective-permute-start.1 = (bf16[2048,128]{1,0:T(8,128)(2,1)S(1)}, bf16[2048,128]{1,0:T(8,128)(2,1)S(1)}, u32[]{:S(2)}, u32[]{:S(2)}) collective-permute-start(bf16[2048,128]{1,0:T(8,128)(2,1)S(1)} %pad_maximum_fusion.1), channel_id=1, source_target_pairs={{0,8},{8,0},{16,24},{24,16},{32,40},{40,32},{48,56},{56,48},{64,72... | collective-permute-start | bytes 1572872 | tf_op jit(solution)/shard_map/ppermute | solution.py:409
  19.4 4.4 %collective-permute-start = (bf16[2048,128]{1,0:T(8,128)(2,1)S(1)}, bf16[2048,128]{1,0:T(8,128)(2,1)S(1)}, u32[]{:S(2)}, u32[]{:S(2)}) collective-permute-start(bf16[2048,128]{1,0:T(8,128)(2,1)S(1)} %pad_maximum_fusion), channel_id=1, source_target_pairs={{0,8},{8,0},{16,24},{24,16},{32,40},{40,32},{48,56},{56,48},{64,72... | collective-permute-start | bytes 1572872 | tf_op jit(solution)/shard_map/ppermute | solution.py:409
  21.3 9.0 %collective-permute-start.2 = (bf16[80,1024]{1,0:T(8,128)(2,1)S(1)}, bf16[80,1024]{1,0:T(8,128)(2,1)S(1)}, u32[]{:S(2)}, u32[]{:S(2)}) collective-permute-start(bf16[80,1024]{1,0:T(8,128)(2,1)S(1)} %bitcast.7), channel_id=1, source_target_pairs={{0,8},{8,0},{16,24},{24,16},{32,40},{40,32},{48,56},{56,48},{64,72... | collective-permute-start | bytes 491528 | tf_op jit(solution)/shard_map/ppermute | solution.py:415
  23.8 0.8 copy-start.4
  23.8 1.0 copy-start.5
  30.3 0.8 copy-start.1
